TPU v7x, 32 devices: a whole 2x2x4 slice. The times are simulated.
32 devices in a mesh: wall: 2 (over x), row: 16 (over z, y, core).
Axes of the slice: x: 2, y: 2, z: 4, core: 2. Of those that a mesh axis runs over, the one named last changes fastest.
Arguments:
- thermal_scalars: float32 [2, 8, 1024, 1024], P(None, 'wall', 'row'), may hold values from -6 to 6
- conductive_number: float32 [2, 8], P(None, 'wall'), may hold values from 0.05 to 0.45
Outputs:
- advanced: float32 [2, 8, 1024, 1024], P(None, 'wall', 'row')
All inputs are finite; a program needn't handle non-finite values.
Results may differ from a plain program's by a relative error of at most 0.00007.
Values sent between devices are 32-bit elements; how exact they have to be, the bound alone decides.
No kernel may reach another device: no remote copies, remote signals or barrier semaphores. Data moves between devices by JAX's collectives and lax.ppermute only.
A program may use at most 64 MiB of HBM per device.

v0:
```python
import functools

import jax
import jax.numpy as jnp
import ml_dtypes
import numpy as np
from jax import lax
from jax.experimental import pallas as pl
from jax.experimental.pallas import tpu as pltpu
from jax.sharding import PartitionSpec as P

STEPS = 3
AXES = ("wall", "row")
LEVELS = 4
VMEM_BYTES = 40 * 1024 * 1024


def cas_table(length, offset, step):
    half = length // 2
    samples = np.arange(half, dtype=np.int64)
    waves = offset + step * np.arange(half, dtype=np.int64)
    angle = (samples[:, None] * waves[None, :] % length) * (2.0 * np.pi / length)
    return np.cos(angle) + np.sin(angle)


def split_table(table):
    high = table.astype(np.float32).astype(ml_dtypes.bfloat16)
    low = (table - high.astype(np.float64)).astype(np.float32).astype(ml_dtypes.bfloat16)
    return np.stack([high, low])


def table_of(length):
    return np.stack([split_table(cas_table(length, parity, 2).T) for parity in range(2)])


def split(value):
    high = value.astype(jnp.bfloat16)
    low = (value - high.astype(jnp.float32)).astype(jnp.bfloat16)
    return high, low


def product(a, b, dims):
    dot = functools.partial(
        lax.dot_general, dimension_numbers=(dims, ((), ())), preferred_element_type=jnp.float32
    )
    return dot(a[0], b[0]) + (dot(a[0], b[1]) + dot(a[1], b[0]))


NN = ((1,), (0,))
NT = ((1,), (1,))


def slot(w, r, groups):
    per_level = groups // LEVELS
    return (w * per_level + r % per_level) * LEVELS + r // per_level


def y_forward_kernel(field_ref, table_ref, out_ref):
    planes, lines, length = field_ref.shape[1:]
    half = length // 2
    rows = planes * lines
    lower = field_ref[0, :, :, :half].reshape(rows, half)
    upper = field_ref[0, :, :, half:].reshape(rows, half)
    folded = jnp.where(pl.program_id(1) == 0, lower + upper, lower - upper)
    waves = product((table_ref[0, 0], table_ref[0, 1]), split(folded), NT)
    out_ref[:, 0] = waves.reshape(out_ref.shape[0], -1, rows)


def y_inverse_kernel(norm, spectrum_ref, table_ref, out_ref):
    devices, _, waves, rows = spectrum_ref.shape
    planes, lines, length = out_ref.shape[1:]
    half = length // 2
    even, odd = (
        product(
            split(spectrum_ref[p * devices // 2 : (p + 1) * devices // 2, 0].reshape(half, rows).T),
            (table_ref[p, 0], table_ref[p, 1]),
            NN,
        )
        for p in range(2)
    )
    out_ref[0, :, :, :half] = ((even + odd) * norm).reshape(planes, lines, half)
    out_ref[0, :, :, half:] = ((even - odd) * norm).reshape(planes, lines, half)


def x_kernel(
    walls, rate_ref, square_y_ref, square_x_ref, table_ref, received_ref, out_ref, sum_ref,
    difference_ref,
):
    devices, _, waves, rows = received_ref.shape
    groups = devices // walls
    scalar = pl.program_id(0)
    half = table_ref.shape[3]
    even_pair, odd_pair = ((table_ref[p, 0], table_ref[p, 1]) for p in range(2))
    lines = 2 * half // groups
    planes = rows // lines
    count = walls * planes
    lower = lax.broadcasted_iota(jnp.int32, (waves, 128), 1) < lines

    def paired(a, b):
        return (
            jnp.where(lower, a, pltpu.roll(b, lines, 1)),
            jnp.where(lower, pltpu.roll(a, lines, 1), b),
        )

    for w in range(walls):
        for p in range(planes // 2):
            lanes = slice(128 * p, 128 * (p + 1))
            top = (w * planes + 2 * p) * waves
            for j in range(groups // 4):
                first, second = 2 * j, 2 * j + groups // 2
                a, b, c, d = (
                    received_ref[slot(w, r, groups), 0, :, lanes]
                    for r in (first, first + 1, second, second + 1)
                )
                columns = slice(128 * j, 128 * (j + 1))
                for target, pieces in (
                    (sum_ref, paired(a + c, b + d)),
                    (difference_ref, paired(a - c, b - d)),
                ):
                    target[top : top + waves, columns] = pieces[0]
                    target[top + waves : top + 2 * waves, columns] = pieces[1]

    sum_ref[...] = product(split(sum_ref[...]), even_pair, NT)
    difference_ref[...] = product(split(difference_ref[...]), odd_pair, NT)

    rates = [rate_ref[scalar, z] for z in range(count)]
    damping_y = [jnp.exp(-rate * square_y_ref[...]) for rate in rates]
    for parity, ref in enumerate((sum_ref, difference_ref)):
        for j in range(half // 128):
            columns = slice(128 * j, 128 * (j + 1))
            square_x = square_x_ref[parity : parity + 1, columns]
            damping = [jnp.exp(-rate * square_x) * dy for rate, dy in zip(rates, damping_y)]
            field = [ref[z * waves : (z + 1) * waves, columns] for z in range(count)]
            for step in range(STEPS):
                updated = []
                for z in range(count):
                    around = field[z - 1] if z > 0 else None
                    if z + 1 < count:
                        around = field[z + 1] if around is None else around + field[z + 1]
                    value = (1.0 - 2.0 * rates[z]) * field[z]
                    if around is not None:
                        value = value + rates[z] * around
                    updated.append(damping[z] * value)
                field = updated
            for z in range(count):
                ref[z * waves : (z + 1) * waves, columns] = field[z]

    even = product(split(sum_ref[...]), even_pair, NN)
    odd = product(split(difference_ref[...]), odd_pair, NN)
    sum_ref[...] = even + odd
    difference_ref[...] = even - odd

    for w in range(walls):
        for p in range(planes // 2):
            lanes = slice(128 * p, 128 * (p + 1))
            top = (w * planes + 2 * p) * waves
            for j in range(groups // 4):
                columns = slice(128 * j, 128 * (j + 1))
                for ref, r in ((sum_ref, 2 * j), (difference_ref, 2 * j + groups // 2)):
                    a, b = paired(
                        ref[top : top + waves, columns],
                        ref[top + waves : top + 2 * waves, columns],
                    )
                    out_ref[slot(w, r, groups), 0, :, lanes] = a
                    out_ref[slot(w, r + 1, groups), 0, :, lanes] = b


PARAMS = pltpu.CompilerParams(vmem_limit_bytes=VMEM_BYTES)
WIDE_PARAMS = pltpu.CompilerParams(vmem_limit_bytes=60 * 1024 * 1024)
VMEM = pl.BlockSpec(memory_space=pltpu.VMEM)


def cost(terms, total):
    return pl.CostEstimate(flops=2 * terms, bytes_accessed=total, transcendentals=0)


def with_kernels(fields, rates, walls, square_y, square_x, y_table, x_table):
    scalars, planes, lines, length = fields.shape
    groups = lax.axis_size("row")
    devices = walls * groups
    waves = length // devices
    rows = planes * lines
    half = length // 2
    blocks = jax.ShapeDtypeStruct((devices, scalars, waves, rows), jnp.float32)
    total = 8 * scalars * rows * length + 2 * length * length
    work = 3 * scalars * rows * length * half
    field_block = pl.BlockSpec((1, planes, lines, length), lambda s, *_: (s, 0, 0, 0))
    spectrum_block = pl.BlockSpec((devices, 1, waves, rows), lambda s: (0, s, 0, 0))

    spectrum = pl.pallas_call(
        y_forward_kernel,
        grid=(scalars, 2),
        in_specs=[field_block, pl.BlockSpec((1, 2, half, half), lambda s, p: (p, 0, 0, 0))],
        out_specs=pl.BlockSpec((devices // 2, 1, waves, rows), lambda s, p: (p, s, 0, 0)),
        out_shape=blocks,
        compiler_params=WIDE_PARAMS,
        cost_estimate=cost(work, total),
        name="y_forward",
    )(fields, y_table)
    filtered = pl.pallas_call(
        functools.partial(x_kernel, walls),
        grid=(scalars,),
        in_specs=[pl.BlockSpec(memory_space=pltpu.SMEM)] + [VMEM] * 3 + [spectrum_block],
        out_specs=spectrum_block,
        out_shape=blocks,
        scratch_shapes=[pltpu.VMEM((walls * planes * waves, x_table.shape[3]), jnp.float32)] * 2,
        compiler_params=PARAMS,
        cost_estimate=cost(2 * work, total),
        name="x_filter",
    )(rates, square_y, square_x, x_table, exchange(spectrum))
    return pl.pallas_call(
        functools.partial(y_inverse_kernel, 1.0 / (length * lines * groups)),
        grid=(scalars,),
        in_specs=[spectrum_block, VMEM],
        out_specs=field_block,
        out_shape=jax.ShapeDtypeStruct(fields.shape, jnp.float32),
        compiler_params=PARAMS,
        cost_estimate=cost(work, total),
        name="y_inverse",
    )(exchange(filtered), y_table)


def exchange(blocks):
    walls, groups = lax.axis_size("wall"), lax.axis_size("row")
    members = {slot(w, r, groups): w * groups + r for w in range(walls) for r in range(groups)}
    return lax.all_to_all(
        blocks, AXES, split_axis=0, concat_axis=0, tiled=True,
        axis_index_groups=[[members[i] for i in range(len(members))]],
    )


def with_arrays(fields, rates, walls, square_y, square_x, y_table, x_table):
    scalars, planes, lines, length = fields.shape
    groups = lax.axis_size("row")
    devices = walls * groups
    waves = length // devices
    count = walls * planes
    order = np.array([slot(w, r, groups) for w in range(walls) for r in range(groups)])
    dot = functools.partial(jnp.matmul, precision=lax.Precision.HIGHEST)

    def whole(table):
        table = jnp.asarray(table)
        return table[0].astype(jnp.float32) + table[1].astype(jnp.float32)

    def forward(value, table):
        half = value.shape[-1] // 2
        a, b = value[..., :half], value[..., half:]
        return jnp.concatenate([dot(a + b, whole(table[0]).T), dot(a - b, whole(table[1]).T)], axis=-1)

    def inverse(value, table):
        half = value.shape[-1] // 2
        even, odd = dot(value[..., :half], whole(table[0])), dot(value[..., half:], whole(table[1]))
        return jnp.concatenate([even + odd, even - odd], axis=-1)

    results = []
    for s in range(scalars):
        spectral = forward(fields[s], y_table).reshape(planes * lines, devices, waves)
        received = exchange(spectral.transpose(1, 2, 0))[order]
        received = received.reshape(walls, groups, waves, planes, lines).transpose(0, 3, 2, 1, 4)
        field = forward(received.reshape(count, waves, groups * lines), x_table)
        rate = rates[s][:, None, None]
        damping = jnp.exp(-rate * (square_y + square_x.reshape(1, -1)))
        for step in range(STEPS):
            padded = jnp.pad(field, ((1, 1), (0, 0), (0, 0)))
            field = damping * (field + rate * (padded[2:] + padded[:-2] - 2.0 * field))
        back = inverse(field, x_table).reshape(walls, planes, waves, groups, lines)
        back = back.transpose(0, 3, 2, 1, 4).reshape(devices, waves, planes * lines)
        spectrum = exchange(back[np.argsort(order)]).reshape(length, -1)
        results.append(inverse(spectrum.T, y_table).reshape(planes, lines, length))
    return jnp.stack(results) * (1.0 / (length * groups * lines))


def signed_square(waves, length):
    signed = jnp.where(waves > length // 2, waves - length, waves)
    scaled = 2.0 * np.pi / length * signed.astype(jnp.float32)
    return scaled * scaled


def per_device(y_table, x_table, thermal_scalars, conductive_number):
    scalars, planes, lines, length = thermal_scalars.shape
    walls, groups = lax.axis_size("wall"), lax.axis_size("row")
    length_x = lines * groups
    devices = walls * groups
    waves = length // devices
    rates = lax.all_gather(conductive_number, "wall", axis=1, tiled=True)
    own = slot(lax.axis_index("wall"), lax.axis_index("row"), groups)
    place = own * waves + jnp.arange(waves, dtype=jnp.int32)
    order = 2 * (place % (length // 2)) + place // (length // 2)
    square_y = signed_square(order, length)[:, None]
    waves_x = jnp.stack([jnp.arange(0, length_x, 2), jnp.arange(1, length_x, 2)])
    square_x = signed_square(waves_x, length_x)
    aligned = lines == 64 and planes % 2 == 0 and waves % 8 == 0 and groups % 4 == 0
    run = with_kernels if aligned else with_arrays
    return run(thermal_scalars, rates, walls, square_y, square_x, y_table, x_table)


def solution(mesh):
    def run(thermal_scalars, conductive_number):
        y_table = table_of(thermal_scalars.shape[3])
        x_table = table_of(thermal_scalars.shape[2])
        return jax.shard_map(
            functools.partial(per_device, y_table, x_table),
            mesh=mesh,
            in_specs=(P(None, "wall", "row", None), P(None, "wall")),
            out_specs=P(None, "wall", "row", None),
            check_vma=False,
        )(thermal_scalars, conductive_number)

    return run
```

profile of v0, /device:TPU:1, one launch (start us, length us, event | category | flops | bytes accessed | tf_op | source)
XLA Modules:
  0.0 122.7 jit_solution(16187198994773588265)
XLA Ops:
  0.0 6.2 %y_forward.1 = f32[32,2,32,256]{3,2,1,0:T(8,128)} custom-call(f32[2,4,64,1024]{3,2,1,0:T(8,128)} %field_ref.1, bf16[2,2,512,512]{3,2,1,0:T(8,128)(2,1)} %constant.77.clone.table_ref), custom_call_target="tpu_custom_call" | custom-call | flops 1610612736 | bytes 6291456 | tf_op jit(solution)/shard_map/y_forward/pallas_call | solution.py:190
  6.2 0.0 copy-start.1
  6.2 0.0 copy-start
  6.2 7.1 %all-to-all-start = ((f32[32,2,32,256]{3,2,1,0:T(8,128)}), f32[32,2,32,256]{3,2,1,0:T(8,128)}, u32[]{:S(2)}, u32[]{:S(2)}) async-start(f32[32,2,32,256]{3,2,1,0:T(8,128)} %y_forward.1), calls=%async_computation | async-start | bytes 4194304 | tf_op jit(solution)/shard_map/all_to_all | solution.py:226
  13.4 0.0 copy-done.1
  13.4 10.4 %all-gather = f32[2,4,2]{1,2,0:T(2,128)S(1)} all-gather(f32[1,4,2]{1,2,0:T(2,128)S(1)} %bitcast.7), channel_id=1, replica_groups=mesh['wall'=2,'row'=16] {'wall'}, dimensions={0}, use_global_device_ids=true | all-gather | bytes 96 | tf_op jit(solution)/shard_map/all_gather | solution.py:285
  23.8 0.1 reshape.107
  23.9 37.7 %all-to-all-done.received_ref = f32[32,2,32,256]{3,2,1,0:T(8,128)} async-done(((f32[32,2,32,256]{3,2,1,0:T(8,128)}), f32[32,2,32,256]{3,2,1,0:T(8,128)}, u32[]{:S(2)}, u32[]{:S(2)}) %all-to-all-start) | async-done | bytes 2097184 | tf_op jit(solution)/shard_map/all_to_all | solution.py:226
  61.7 0.0 copy-done
  61.7 6.0 %x_filter.1 = f32[32,2,32,256]{3,2,1,0:T(8,128)S(1)} custom-call(f32[2,8]{1,0:T(2,128)S(1)} %bitcast.6, f32[32,1]{1,0:T(8,128)S(1)} %fusion.4.square_y_ref, f32[2,512]{1,0:T(2,128)S(1)} %fusion.12.square_x_ref, bf16[2,2,512,512]{3,2,1,0:T(8,128)(2,1)S(1)} %copy-done, f32[32,2,32,256]{3,2,1,0:T(8,128)} %all-to-all-done.received_ref), custom_call_target="tpu_custom_call" | custom-call | flops 3221225472 | bytes 6291456 | tf_op jit(solution)/shard_map/x_filter/pallas_call | solution.py:200
  67.7 51.8 %all_to_all.10.spectrum_ref = f32[32,2,32,256]{3,2,1,0:T(8,128)S(1)} all-to-all(f32[32,2,32,256]{3,2,1,0:T(8,128)S(1)} %x_filter.1), channel_id=1, replica_groups={{0,4,8,12,1,5,9,13,2,6,10,14,3,7,11,15,16,20,24,28,17,21,25,29,18,22,26..., dimensions={0} | all-to-all | bytes 4194304 | tf_op jit(solution)/shard_map/all_to_all | solution.py:226
  119.5 3.2 %y_inverse.1 = f32[2,4,64,1024]{3,2,1,0:T(8,128)} custom-call(f32[32,2,32,256]{3,2,1,0:T(8,128)S(1)} %all_to_all.10.spectrum_ref, bf16[2,2,512,512]{3,2,1,0:T(8,128)(2,1)S(1)} %copy-done), custom_call_target="tpu_custom_call" | custom-call | flops 1610612736 | bytes 6291456 | tf_op jit(solution)/shard_map/y_inverse/pallas_call | solution.py:211
  (4 shorter events, 0.1 us)
Async XLA Ops:
  6.2 7.2 %copy-start.1 = (f32[2,4]{1,0:T(2,128)S(1)}, f32[2,4]{1,0:T(2,128)}, u32[]{:S(2)}) copy-start(f32[2,4]{1,0:T(2,128)} %param.5) | copy-start | bytes 100
  6.2 55.5 %copy-start = (bf16[2,2,512,512]{3,2,1,0:T(8,128)(2,1)S(1)}, bf16[2,2,512,512]{3,2,1,0:T(8,128)(2,1)}, u32[]{:S(2)}) copy-start(bf16[2,2,512,512]{3,2,1,0:T(8,128)(2,1)} %constant.77.clone.table_ref) | copy-start | bytes 6291460
  6.2 55.5 %all-to-all-start = ((f32[32,2,32,256]{3,2,1,0:T(8,128)}), f32[32,2,32,256]{3,2,1,0:T(8,128)}, u32[]{:S(2)}, u32[]{:S(2)}) async-start(f32[32,2,32,256]{3,2,1,0:T(8,128)} %y_forward.1), calls=%async_computation | async-start | bytes 4194304 | tf_op jit(solution)/shard_map/all_to_all | solution.py:226
where the time goes:
time: 123 us
  blocking collectives  62.2 us (51%)
  waiting for transfers between devices  37.7 us (31%)
  Pallas kernels  15.4 us (13%)
  starting transfers between devices  7.15 us (6%)
    all_to_all x1, blocking collectives, exchange(): lax.all_to_all(blocks, AXES, split_axis=0, concat_axis=0, tiled=True, axi...  51.8 us
    all_to_all x1, waiting for transfers between devices, exchange(): lax.all_to_all(blocks, AXES, split_axis=0, concat_axis=0, tiled=True, axi...  37.7 us
    all_gather x1, blocking collectives, per_device(): rates = lax.all_gather(conductive_number, 'wall', axis=1, tiled=True)  10.4 us
    all_to_all x1, starting transfers between devices, exchange(): lax.all_to_all(blocks, AXES, split_axis=0, concat_axis=0, tiled=True, axi...  7.15 us
    pallas_call x1, Pallas kernels, with_kernels(): pl.pallas_call(y_forward_kernel, grid=(scalars, 2), in_specs=[field_block...  6.21 us
    pallas_call x1, Pallas kernels, with_kernels(): pl.pallas_call(functools.partial(x_kernel, walls), grid=(scalars,), in_sp...  6.03 us
    pallas_call x1, Pallas kernels, with_kernels(): pl.pallas_call(functools.partial(y_inverse_kernel, 1.0 / (length * lines...  3.2 us
  transfers between devices with their start and end apart: 1, of which 1 were waited for; matrix products, arithmetic and copies ran while one was open for 0% of the time, Pallas kernels for 0%

commit v1 on v0

--- a/solution.py
+++ b/solution.py
@@ -12,6 +12,7 @@
 STEPS = 3
 AXES = ("wall", "row")
 LEVELS = 4
+PARTS = 4
 VMEM_BYTES = 40 * 1024 * 1024
 
 
@@ -40,10 +41,9 @@
 
 
 def product(a, b, dims):
-    dot = functools.partial(
-        lax.dot_general, dimension_numbers=(dims, ((), ())), preferred_element_type=jnp.float32
-    )
-    return dot(a[0], b[0]) + (dot(a[0], b[1]) + dot(a[1], b[0]))
+    left = jnp.concatenate([a[0], a[1], a[0]], axis=dims[0][0])
+    right = jnp.concatenate([b[0], b[0], b[1]], axis=dims[1][0])
+    return lax.dot_general(left, right, (dims, ((), ())), preferred_element_type=jnp.float32)
 
 
 NN = ((1,), (0,))
@@ -55,24 +55,25 @@
     return (w * per_level + r % per_level) * LEVELS + r // per_level
 
 
-def y_forward_kernel(field_ref, table_ref, out_ref):
-    planes, lines, length = field_ref.shape[1:]
-    half = length // 2
+def y_forward_kernel(lower_ref, upper_ref, high_ref, low_ref, out_ref):
+    planes, lines, half = lower_ref.shape[1:]
     rows = planes * lines
-    lower = field_ref[0, :, :, :half].reshape(rows, half)
-    upper = field_ref[0, :, :, half:].reshape(rows, half)
+    lower = lower_ref[0].reshape(rows, half)
+    upper = upper_ref[0].reshape(rows, half)
     folded = jnp.where(pl.program_id(1) == 0, lower + upper, lower - upper)
-    waves = product((table_ref[0, 0], table_ref[0, 1]), split(folded), NT)
+    waves = product((high_ref[0, 0], low_ref[0, 0]), split(folded), NT)
     out_ref[:, 0] = waves.reshape(out_ref.shape[0], -1, rows)
 
 
-def y_inverse_kernel(norm, spectrum_ref, table_ref, out_ref):
-    devices, _, waves, rows = spectrum_ref.shape
+def y_inverse_kernel(norm, *refs):
+    spectrum_refs, (table_ref, out_ref) = refs[:-2], refs[-2:]
+    rows = spectrum_refs[0].shape[3]
+    share = len(spectrum_refs) // 2
     planes, lines, length = out_ref.shape[1:]
     half = length // 2
     even, odd = (
         product(
-            split(spectrum_ref[p * devices // 2 : (p + 1) * devices // 2, 0].reshape(half, rows).T),
+            split(jnp.concatenate([ref[:, 0].reshape(-1, rows) for ref in spectrum_refs[p * share : (p + 1) * share]]).T),
             (table_ref[p, 0], table_ref[p, 1]),
             NN,
         )
@@ -83,11 +84,12 @@
 
 
 def x_kernel(
-    walls, rate_ref, square_y_ref, square_x_ref, table_ref, received_ref, out_ref, sum_ref,
-    difference_ref,
+    walls, rate_ref, square_y_ref, square_x_ref, table_ref, *refs
 ):
-    devices, _, waves, rows = received_ref.shape
+    received_refs, (out_ref, sum_ref, difference_ref) = refs[:-3], refs[-3:]
+    devices, _, waves, rows = out_ref.shape
     groups = devices // walls
+    part = devices // len(received_refs)
     scalar = pl.program_id(0)
     half = table_ref.shape[3]
     even_pair, odd_pair = ((table_ref[p, 0], table_ref[p, 1]) for p in range(2))
@@ -109,8 +111,8 @@
             for j in range(groups // 4):
                 first, second = 2 * j, 2 * j + groups // 2
                 a, b, c, d = (
-                    received_ref[slot(w, r, groups), 0, :, lanes]
-                    for r in (first, first + 1, second, second + 1)
+                    received_refs[i // part][i % part, 0, :, lanes]
+                    for i in (slot(w, r, groups) for r in (first, first + 1, second, second + 1))
                 )
                 columns = slice(128 * j, 128 * (j + 1))
                 for target, pieces in (
@@ -184,40 +186,50 @@
     blocks = jax.ShapeDtypeStruct((devices, scalars, waves, rows), jnp.float32)
     total = 8 * scalars * rows * length + 2 * length * length
     work = 3 * scalars * rows * length * half
-    field_block = pl.BlockSpec((1, planes, lines, length), lambda s, *_: (s, 0, 0, 0))
+    field_block = pl.BlockSpec((1, planes, lines, length), lambda s: (s, 0, 0, 0))
     spectrum_block = pl.BlockSpec((devices, 1, waves, rows), lambda s: (0, s, 0, 0))
+
+    part_blocks = [
+        pl.BlockSpec((devices // PARTS, 1, waves, rows), lambda s, i=i: (i, s, 0, 0)) for i in range(PARTS)
+    ]
 
     spectrum = pl.pallas_call(
         y_forward_kernel,
         grid=(scalars, 2),
-        in_specs=[field_block, pl.BlockSpec((1, 2, half, half), lambda s, p: (p, 0, 0, 0))],
+        in_specs=[
+            pl.BlockSpec((1, planes, lines, half), lambda s, p, i=i: (s, 0, 0, i)) for i in range(2)
+        ] + [
+            pl.BlockSpec((1, 1, half, half), lambda s, p, i=i: (p, i, 0, 0)) for i in range(2)
+        ],
         out_specs=pl.BlockSpec((devices // 2, 1, waves, rows), lambda s, p: (p, s, 0, 0)),
         out_shape=blocks,
         compiler_params=WIDE_PARAMS,
         cost_estimate=cost(work, total),
         name="y_forward",
-    )(fields, y_table)
+    )(fields, fields, y_table, y_table)
+    received = exchange(spectrum)
     filtered = pl.pallas_call(
         functools.partial(x_kernel, walls),
         grid=(scalars,),
-        in_specs=[pl.BlockSpec(memory_space=pltpu.SMEM)] + [VMEM] * 3 + [spectrum_block],
+        in_specs=[pl.BlockSpec(memory_space=pltpu.SMEM)] + [VMEM] * 3 + part_blocks,
         out_specs=spectrum_block,
         out_shape=blocks,
         scratch_shapes=[pltpu.VMEM((walls * planes * waves, x_table.shape[3]), jnp.float32)] * 2,
         compiler_params=PARAMS,
         cost_estimate=cost(2 * work, total),
         name="x_filter",
-    )(rates, square_y, square_x, x_table, exchange(spectrum))
+    )(rates, square_y, square_x, x_table, *[received] * PARTS)
+    returned = exchange(filtered)
     return pl.pallas_call(
         functools.partial(y_inverse_kernel, 1.0 / (length * lines * groups)),
         grid=(scalars,),
-        in_specs=[spectrum_block, VMEM],
+        in_specs=part_blocks + [VMEM],
         out_specs=field_block,
         out_shape=jax.ShapeDtypeStruct(fields.shape, jnp.float32),
         compiler_params=PARAMS,
         cost_estimate=cost(work, total),
         name="y_inverse",
-    )(exchange(filtered), y_table)
+    )(*[returned] * PARTS, y_table)
 
 
 def exchange(blocks):

time: 123 us -> 124 us (level)
  local copies, waits for them, and re-layouts: 0.09 us -> 1.68 us
    unnamed x5, local copies, waits for them, and re-layouts: 0.09 us -> 1.68 us
where the time goes in v1:
time: 124 us
  blocking collectives  62.2 us (50%)
  waiting for transfers between devices  37.7 us (30%)
  Pallas kernels  14.9 us (12%)
  starting transfers between devices  7.09 us (6%)
  local copies, waits for them, and re-layouts  1.68 us (1%)
    all_to_all x1, blocking collectives, exchange(): lax.all_to_all(blocks, AXES, split_axis=0, concat_axis=0, tiled=True, axi...  51.8 us
    all_to_all x1, waiting for transfers between devices, exchange(): lax.all_to_all(blocks, AXES, split_axis=0, concat_axis=0, tiled=True, axi...  37.7 us
    all_gather x1, blocking collectives, per_device(): rates = lax.all_gather(conductive_number, 'wall', axis=1, tiled=True)  10.4 us
    all_to_all x1, starting transfers between devices, exchange(): lax.all_to_all(blocks, AXES, split_axis=0, concat_axis=0, tiled=True, axi...  7.09 us
    pallas_call x1, Pallas kernels, with_kernels(): pl.pallas_call(y_forward_kernel, grid=(scalars, 2), in_specs=[pl.BlockSpe...  6.14 us
    pallas_call x1, Pallas kernels, with_kernels(): pl.pallas_call(functools.partial(x_kernel, walls), grid=(scalars,), in_sp...  5.6 us
    pallas_call x1, Pallas kernels, with_kernels(): pl.pallas_call(functools.partial(y_inverse_kernel, 1.0 / (length * lines...  3.21 us
  transfers between devices with their start and end apart: 1, of which 1 were waited for; matrix products, arithmetic and copies ran while one was open for 0% of the time, Pallas kernels for 0%

profile of v1, /device:TPU:1, one launch (start us, length us, event | category | flops | bytes accessed | tf_op | source)
XLA Modules:
  0.0 123.7 jit_solution(17411650509262592594)
XLA Ops:
  0.0 6.1 %y_forward.1 = f32[32,2,32,256]{3,2,1,0:T(8,128)} custom-call(f32[2,4,64,1024]{3,2,1,0:T(8,128)} %upper_ref.1, f32[2,4,64,1024]{3,2,1,0:T(8,128)} %upper_ref.1, bf16[2,2,512,512]{3,2,1,0:T(8,128)(2,1)} %constant.77.clone.high_ref.low_ref.table_ref.refs_4_, bf16[2,2,512,512]{3,2,1,0:T(8,128)(2,1)} %constant.77.clone.high_ref.low_ref.table_ref.refs_4_), custom_call_target="tpu_custom_call" | custom-call | flops 1610612736 | bytes 6291456 | tf_op jit(solution)/shard_map/y_forward/pallas_call | solution.py:196
  6.1 0.0 copy-start.1
  6.1 7.1 %all-to-all-start = ((f32[32,2,32,256]{3,2,1,0:T(8,128)}), f32[32,2,32,256]{3,2,1,0:T(8,128)S(1)}, u32[]{:S(2)}, u32[]{:S(2)}) async-start(f32[32,2,32,256]{3,2,1,0:T(8,128)} %y_forward.1), calls=%async_computation | async-start | bytes 4194304 | tf_op jit(solution)/shard_map/all_to_all | solution.py:238
  13.2 0.0 copy-done.1
  13.3 10.4 %all-gather = f32[2,4,2]{1,2,0:T(2,128)S(1)} all-gather(f32[1,4,2]{1,2,0:T(2,128)S(1)} %bitcast.7), channel_id=1, replica_groups=mesh['wall'=2,'row'=16] {'wall'}, dimensions={0}, use_global_device_ids=true | all-gather | bytes 96 | tf_op jit(solution)/shard_map/all_gather | solution.py:297
  23.6 0.1 reshape.107
  23.8 37.7 %all-to-all-done.refs_0_.refs_1_.refs_2_.refs_3_ = f32[32,2,32,256]{3,2,1,0:T(8,128)S(1)} async-done(((f32[32,2,32,256]{3,2,1,0:T(8,128)}), f32[32,2,32,256]{3,2,1,0:T(8,128)S(1)}, u32[]{:S(2)}, u32[]{:S(2)}) %all-to-all-start) | async-done | bytes 2097184 | tf_op jit(solution)/shard_map/all_to_all | solution.py:238
  61.5 0.0 copy-start
  61.5 1.6 %copy-done = bf16[2,2,512,512]{3,2,1,0:T(8,128)(2,1)S(1)} copy-done((bf16[2,2,512,512]{3,2,1,0:T(8,128)(2,1)S(1)}, bf16[2,2,512,512]{3,2,1,0:T(8,128)(2,1)}, u32[]{:S(2)}) %copy-start) | copy-done | bytes 2097176
  63.1 5.6 %x_filter.1 = f32[32,2,32,256]{3,2,1,0:T(8,128)S(1)} custom-call(f32[2,8]{1,0:T(2,128)S(1)} %bitcast.6, f32[32,1]{1,0:T(8,128)S(1)} %fusion.4.square_y_ref, f32[2,512]{1,0:T(2,128)S(1)} %fusion.12.square_x_ref, bf16[2,2,512,512]{3,2,1,0:T(8,128)(2,1)S(1)} %copy-done, f32[32,2,32,256]{3,2,1,0:T(8,128)S(1)} %all-to-all-done.refs_0_.refs_1_.refs_2_.refs_3_, ...), custom_call_target="tpu_custom_call" | custom-call | flops 3221225472 | bytes 6291456 | tf_op jit(solution)/shard_map/x_filter/pallas_call | solution.py:211
  68.7 51.8 %all_to_all.10.refs_0_.refs_1_.refs_2_.refs_3_ = f32[32,2,32,256]{3,2,1,0:T(8,128)S(1)} all-to-all(f32[32,2,32,256]{3,2,1,0:T(8,128)S(1)} %x_filter.1), channel_id=1, replica_groups={{0,4,8,12,1,5,9,13,2,6,10,14,3,7,11,15,16,20,24,28,17,21,25,29,18,22,26..., dimensions={0} | all-to-all | bytes 4194304 | tf_op jit(solution)/shard_map/all_to_all | solution.py:238
  120.5 3.2 %y_inverse.1 = f32[2,4,64,1024]{3,2,1,0:T(8,128)} custom-call(f32[32,2,32,256]{3,2,1,0:T(8,128)S(1)} %all_to_all.10.refs_0_.refs_1_.refs_2_.refs_3_, f32[32,2,32,256]{3,2,1,0:T(8,128)S(1)} %all_to_all.10.refs_0_.refs_1_.refs_2_.refs_3_, f32[32,2,32,256]{3,2,1,0:T(8,128)S(1)} %all_to_all.10.refs_0_.refs_1_.refs_2_.refs_3_, ...), custom_call_target="tpu_custom_call" | custom-call | flops 1610612736 | bytes 6291456 | tf_op jit(solution)/shard_map/y_inverse/pallas_call | solution.py:223
  (4 shorter events, 0.1 us)
Async XLA Ops:
  6.1 7.1 %copy-start.1 = (f32[2,4]{1,0:T(2,128)S(1)}, f32[2,4]{1,0:T(2,128)}, u32[]{:S(2)}) copy-start(f32[2,4]{1,0:T(2,128)} %param.5) | copy-start | bytes 100
  6.1 55.4 %all-to-all-start = ((f32[32,2,32,256]{3,2,1,0:T(8,128)}), f32[32,2,32,256]{3,2,1,0:T(8,128)S(1)}, u32[]{:S(2)}, u32[]{:S(2)}) async-start(f32[32,2,32,256]{3,2,1,0:T(8,128)} %y_forward.1), calls=%async_computation | async-start | bytes 4194304 | tf_op jit(solution)/shard_map/all_to_all | solution.py:238
  61.5 1.6 %copy-start = (bf16[2,2,512,512]{3,2,1,0:T(8,128)(2,1)S(1)}, bf16[2,2,512,512]{3,2,1,0:T(8,128)(2,1)}, u32[]{:S(2)}) copy-start(bf16[2,2,512,512]{3,2,1,0:T(8,128)(2,1)} %constant.77.clone.high_ref.low_ref.table_ref.refs_4_) | copy-start | bytes 6291460

commit v2 on v0

v2 whole, which is shorter than its diff:
```python
import functools

import jax
import jax.numpy as jnp
import ml_dtypes
import numpy as np
from jax import lax
from jax.experimental import pallas as pl
from jax.experimental.pallas import tpu as pltpu
from jax.sharding import PartitionSpec as P

STEPS = 3
AXES = ("wall", "row")
LEVELS = 4
VMEM_BYTES = 40 * 1024 * 1024


def wave_order(place, length):
    quarter = length // 4
    even = jnp.where(place < quarter, 4 * place, 4 * (place - quarter) + 2)
    return jnp.where(place < 2 * quarter, even, 2 * (place - 2 * quarter) + 1)


def cas_table(length, first, step):
    size = length // step
    waves = first + step * np.arange(size, dtype=np.int64)
    samples = np.arange(size, dtype=np.int64)
    angle = (waves[:, None] * samples[None, :] % length) * (2.0 * np.pi / length)
    table = np.cos(angle) + np.sin(angle)
    high = table.astype(np.float32).astype(ml_dtypes.bfloat16)
    low = (table - high.astype(np.float64)).astype(np.float32).astype(ml_dtypes.bfloat16)
    return np.stack([high, low])


def tables_of(length):
    even = np.stack([cas_table(length, 0, 4), cas_table(length, 2, 4)])
    return even, cas_table(length, 1, 2)


def fold(q):
    low, high = q[0] + q[2], q[1] + q[3]
    return low + high, low - high, q[0] - q[2], q[1] - q[3]


def unfold(first, second, third, fourth):
    low, high = first + second, first - second
    return low + third, high + fourth, low - third, high - fourth


def split(value):
    high = value.astype(jnp.bfloat16)
    low = (value - high.astype(jnp.float32)).astype(jnp.bfloat16)
    return high, low


def product(a, b, dims):
    left = jnp.concatenate([a[0], a[1], a[0]], axis=dims[0][0])
    right = jnp.concatenate([b[0], b[0], b[1]], axis=dims[1][0])
    return lax.dot_general(left, right, (dims, ((), ())), preferred_element_type=jnp.float32)


NN = ((1,), (0,))
NT = ((1,), (1,))


def part_tables(even_ref, odd_ref):
    return [(even_ref[p, 0], even_ref[p, 1]) for p in range(2)] + [(odd_ref[0], odd_ref[1])]


def part_ranges(total):
    return (0, total // 4), (total // 4, total // 2), (total // 2, total)


def slot(w, r, groups):
    per_level = groups // LEVELS
    return (w * per_level + r % per_level) * LEVELS + r // per_level


def y_forward_kernel(
    field_hbm, even_hbm, odd_hbm, out_hbm, even_ref, odd_ref, field_ref, out_ref, in_sem, table_sem,
    out_sem,
):
    scalars, planes, lines, length = field_ref.shape
    rows = planes * lines
    quarter = length // 4
    loads = [
        pltpu.make_async_copy(field_hbm.at[s], field_ref.at[s], in_sem.at[s]) for s in range(scalars)
    ]
    even_load = pltpu.make_async_copy(even_hbm, even_ref, table_sem.at[0])
    odd_load = pltpu.make_async_copy(odd_hbm, odd_ref, table_sem.at[1])
    loads[0].start()
    even_load.start()
    odd_load.start()
    for load in loads[1:]:
        load.start()
    stores = []
    for s in range(scalars):
        loads[s].wait()
        lines_of = [
            field_ref[s, :, :, q * quarter : (q + 1) * quarter].reshape(rows, quarter) for q in range(4)
        ]
        first, second, third, fourth = fold(lines_of)
        parts = [first, second, jnp.concatenate([third, fourth], axis=1)]
        for p, (low, high) in enumerate(part_ranges(out_ref.shape[0])):
            if s == 0 and p == 0:
                even_load.wait()
            if s == 0 and p == 2:
                odd_load.wait()
            table = (odd_ref[0], odd_ref[1]) if p == 2 else (even_ref[p, 0], even_ref[p, 1])
            waves = product(table, split(parts[p]), NT)
            out_ref[low:high, s] = waves.reshape(high - low, -1, rows)
            store = pltpu.make_async_copy(
                out_ref.at[pl.ds(low, high - low), s],
                out_hbm.at[pl.ds(low, high - low), s],
                out_sem.at[s, p],
            )
            store.start()
            stores.append(store)
    for store in stores:
        store.wait()


def y_inverse_kernel(norm, even_ref, odd_ref, spectrum_ref, out_hbm, out_ref, out_sem):
    devices, scalars, waves, rows = spectrum_ref.shape
    planes, lines, length = out_ref.shape[1:]
    quarter = length // 4
    tables = part_tables(even_ref, odd_ref)
    stores = []
    for s in range(scalars):
        first, second, third = (
            product(split(spectrum_ref[low:high, s].reshape(-1, rows).T), table, NN)
            for table, (low, high) in zip(tables, part_ranges(devices))
        )
        quarters = unfold(first * norm, second * norm, third[:, :quarter] * norm, third[:, quarter:] * norm)
        for q, value in enumerate(quarters):
            out_ref[s, :, :, q * quarter : (q + 1) * quarter] = value.reshape(planes, lines, quarter)
        for z in range(planes):
            store = pltpu.make_async_copy(out_ref.at[s, z], out_hbm.at[s, z], out_sem.at[s, z])
            store.start()
            stores.append(store)
    for store in stores:
        store.wait()


def x_kernel(
    walls, rate_ref, square_y_ref, square_x_ref, even_ref, odd_ref, received_ref, out_ref, *line_refs
):
    devices, scalars, waves, rows = received_ref.shape
    groups = devices // walls
    length = line_refs[0].shape[1]
    quarter = length // 4
    lines = length // groups
    planes = rows // lines
    count = walls * planes
    lower = lax.broadcasted_iota(jnp.int32, (waves, 128), 1) < lines
    tables = part_tables(even_ref, odd_ref)
    ranges = part_ranges(length)

    def paired(a, b):
        return (
            jnp.where(lower, a, pltpu.roll(b, lines, 1)),
            jnp.where(lower, pltpu.roll(a, lines, 1), b),
        )

    def tiles():
        for w in range(walls):
            for p in range(planes // 2):
                yield w, slice(128 * p, 128 * (p + 1)), (w * planes + 2 * p) * waves

    def forward(s):
        line_ref = line_refs[s]
        for w, lanes, top in tiles():
            for i in range(groups // 8):
                left, right = (
                    fold([
                        received_ref[slot(w, groups // 4 * q + 2 * i + side, groups), s, :, lanes]
                        for q in range(4)
                    ])
                    for side in range(2)
                )
                for q in range(4):
                    a, b = paired(left[q], right[q])
                    columns = slice(quarter * q + 128 * i, quarter * q + 128 * (i + 1))
                    line_ref[top : top + waves, columns] = a
                    line_ref[top + waves : top + 2 * waves, columns] = b
        for table, (low, high) in zip(tables, ranges):
            line_ref[:, low:high] = product(split(line_ref[:, low:high]), table, NT)

    def diffuse(s):
        line_ref = line_refs[s]
        rates = [rate_ref[s, z] for z in range(count)]
        damping_y = [jnp.exp(-rate * square_y_ref[...]) for rate in rates]
        for j in range(length // 128):
            columns = slice(128 * j, 128 * (j + 1))
            square_x = square_x_ref[:, columns]
            damping = [jnp.exp(-rate * square_x) * dy for rate, dy in zip(rates, damping_y)]
            field = [line_ref[z * waves : (z + 1) * waves, columns] for z in range(count)]
            for step in range(STEPS):
                updated = []
                for z in range(count):
                    value = (1.0 - 2.0 * rates[z]) * field[z]
                    if z == 0:
                        around = field[1]
                    elif z == count - 1:
                        around = field[z - 1]
                    else:
                        around = field[z - 1] + field[z + 1]
                    updated.append(damping[z] * (value + rates[z] * around))
                field = updated
            for z in range(count):
                line_ref[z * waves : (z + 1) * waves, columns] = field[z]

    def inverse(s):
        line_ref = line_refs[s]
        first, second, third = (
            product(split(line_ref[:, low:high]), table, NN) for table, (low, high) in zip(tables, ranges)
        )
        quarters = unfold(first, second, third[:, :quarter], third[:, quarter:])
        for q, value in enumerate(quarters):
            line_ref[:, q * quarter : (q + 1) * quarter] = value
        for w, lanes, top in tiles():
            for j in range(groups // 2):
                columns = slice(128 * j, 128 * (j + 1))
                a, b = paired(
                    line_ref[top : top + waves, columns],
                    line_ref[top + waves : top + 2 * waves, columns],
                )
                out_ref[slot(w, 2 * j, groups), s, :, lanes] = a
                out_ref[slot(w, 2 * j + 1, groups), s, :, lanes] = b

    for phase in (forward, diffuse, inverse):
        for s in range(scalars):
            phase(s)


PARAMS = pltpu.CompilerParams(vmem_limit_bytes=VMEM_BYTES)
VMEM = pl.BlockSpec(memory_space=pltpu.VMEM)
ANY = pl.BlockSpec(memory_space=pl.ANY)


def cost(terms, total):
    return pl.CostEstimate(flops=2 * terms, bytes_accessed=total, transcendentals=0)


def with_kernels(fields, rates, walls, square_y, square_x, tables):
    scalars, planes, lines, length = fields.shape
    groups = lax.axis_size("row")
    devices = walls * groups
    waves = length // devices
    rows = planes * lines
    even, odd = tables
    blocks = jax.ShapeDtypeStruct((devices, scalars, waves, rows), jnp.float32)
    shapes = [jax.ShapeDtypeStruct(t.shape, jnp.bfloat16) for t in tables]
    total = 8 * scalars * rows * length
    work = 9 * scalars * rows * length * length // 8

    spectrum, even, odd = pl.pallas_call(
        y_forward_kernel,
        in_specs=[ANY] * 3,
        out_specs=[ANY, VMEM, VMEM],
        out_shape=[blocks, *shapes],
        scratch_shapes=[
            pltpu.VMEM(fields.shape, jnp.float32),
            pltpu.VMEM(blocks.shape, jnp.float32),
            pltpu.SemaphoreType.DMA((scalars,)),
            pltpu.SemaphoreType.DMA((2,)),
            pltpu.SemaphoreType.DMA((scalars, 3)),
        ],
        compiler_params=PARAMS,
        cost_estimate=cost(work, total),
        name="y_forward",
    )(fields, even, odd)
    filtered = pl.pallas_call(
        functools.partial(x_kernel, walls),
        in_specs=[pl.BlockSpec(memory_space=pltpu.SMEM)] + [VMEM] * 5,
        out_specs=VMEM,
        out_shape=blocks,
        scratch_shapes=[pltpu.VMEM((walls * planes * waves, lines * groups), jnp.float32)] * scalars,
        compiler_params=PARAMS,
        cost_estimate=cost(2 * work, total),
        name="x_filter",
    )(rates, square_y, square_x, even, odd, exchange(spectrum))
    return pl.pallas_call(
        functools.partial(y_inverse_kernel, 1.0 / (length * lines * groups)),
        in_specs=[VMEM] * 3,
        out_specs=ANY,
        out_shape=jax.ShapeDtypeStruct(fields.shape, jnp.float32),
        scratch_shapes=[
            pltpu.VMEM(fields.shape, jnp.float32),
            pltpu.SemaphoreType.DMA((scalars, planes)),
        ],
        compiler_params=PARAMS,
        cost_estimate=cost(work, total),
        name="y_inverse",
    )(even, odd, exchange(filtered))


def exchange(blocks):
    walls, groups = lax.axis_size("wall"), lax.axis_size("row")
    members = {slot(w, r, groups): w * groups + r for w in range(walls) for r in range(groups)}
    return lax.all_to_all(
        blocks, AXES, split_axis=0, concat_axis=0, tiled=True,
        axis_index_groups=[[members[i] for i in range(len(members))]],
    )


def with_arrays(fields, rates, walls, square_y, square_x, y_tables, x_tables):
    scalars, planes, lines, length = fields.shape
    groups = lax.axis_size("row")
    devices = walls * groups
    waves = length // devices
    count = walls * planes
    order = np.array([slot(w, r, groups) for w in range(walls) for r in range(groups)])
    dot = functools.partial(jnp.matmul, precision=lax.Precision.HIGHEST)

    def whole(tables):
        pairs = [jnp.asarray(t).astype(jnp.float32) for t in (*tables[0], tables[1])]
        return [t[0] + t[1] for t in pairs]

    def forward(value, tables):
        first, second, third, fourth = fold(jnp.split(value, 4, axis=-1))
        parts = (first, second, jnp.concatenate([third, fourth], axis=-1))
        return jnp.concatenate([dot(v, t.T) for v, t in zip(parts, whole(tables))], axis=-1)

    def inverse(value, tables):
        parts = jnp.split(value, [value.shape[-1] // 4, value.shape[-1] // 2], axis=-1)
        first, second, third = (dot(v, t) for v, t in zip(parts, whole(tables)))
        return jnp.concatenate(unfold(first, second, *jnp.split(third, 2, axis=-1)), axis=-1)

    results = []
    for s in range(scalars):
        spectral = forward(fields[s], y_tables).reshape(planes * lines, devices, waves)
        received = exchange(spectral.transpose(1, 2, 0))[order]
        received = received.reshape(walls, groups, waves, planes, lines).transpose(0, 3, 2, 1, 4)
        field = forward(received.reshape(count, waves, groups * lines), x_tables)
        rate = rates[s][:, None, None]
        damping = jnp.exp(-rate * (square_y + square_x))
        for step in range(STEPS):
            padded = jnp.pad(field, ((1, 1), (0, 0), (0, 0)))
            field = damping * (field + rate * (padded[2:] + padded[:-2] - 2.0 * field))
        back = inverse(field, x_tables).reshape(walls, planes, waves, groups, lines)
        back = back.transpose(0, 3, 2, 1, 4).reshape(devices, waves, planes * lines)
        spectrum = exchange(back[np.argsort(order)]).reshape(length, -1)
        results.append(inverse(spectrum.T, y_tables).reshape(planes, lines, length))
    return jnp.stack(results) * (1.0 / (length * groups * lines))


def signed_square(waves, length):
    signed = jnp.where(waves > length // 2, waves - length, waves)
    scaled = 2.0 * np.pi / length * signed.astype(jnp.float32)
    return scaled * scaled


def per_device(thermal_scalars, conductive_number):
    scalars, planes, lines, length = thermal_scalars.shape
    walls, groups = lax.axis_size("wall"), lax.axis_size("row")
    length_x = lines * groups
    waves = length // (walls * groups)
    rates = lax.all_gather(conductive_number, "wall", axis=1, tiled=True)
    own = slot(lax.axis_index("wall"), lax.axis_index("row"), groups)
    place = own * waves + jnp.arange(waves, dtype=jnp.int32)
    square_y = signed_square(wave_order(place, length), length)[:, None]
    square_x = signed_square(wave_order(jnp.arange(length_x), length_x), length_x)[None, :]
    fits = lines == 64 and planes % 2 == 0 and waves % 8 == 0 and groups % 8 == 0
    if fits and length == length_x and walls * groups % 4 == 0:
        return with_kernels(thermal_scalars, rates, walls, square_y, square_x, tables_of(length))
    return with_arrays(
        thermal_scalars, rates, walls, square_y, square_x, tables_of(length), tables_of(length_x)
    )


def solution(mesh):
    return jax.shard_map(
        per_device,
        mesh=mesh,
        in_specs=(P(None, "wall", "row", None), P(None, "wall")),
        out_specs=P(None, "wall", "row", None),
        check_vma=False,
    )
```

time: 123 us -> 125 us (1.016)
  local copies, waits for them, and re-layouts: 0.09 us -> 7.1 us
  Pallas kernels: 15.4 us -> 10.8 us
    unnamed x5 -> x15, local copies, waits for them, and re-layouts: 0.09 us -> 7.1 us
    pallas_call x2, Pallas kernels: 12.2 us -> 8.16 us  [the longest x1 4.15 us: with_kernels(): pl.pallas_call(functools.partial(x_kernel, walls), in_specs=[pl.BlockSpec...]
where the time goes in v2:
time: 125 us
  blocking collectives  62.2 us (50%)
  waiting for transfers between devices  37.8 us (30%)
  Pallas kernels  10.8 us (9%)
  local copies, waits for them, and re-layouts  7.1 us (6%)
  starting transfers between devices  7.1 us (6%)
    all_to_all x1, blocking collectives, exchange(): lax.all_to_all(blocks, AXES, split_axis=0, concat_axis=0, tiled=True, axi...  51.8 us
    all_to_all x1, waiting for transfers between devices, exchange(): lax.all_to_all(blocks, AXES, split_axis=0, concat_axis=0, tiled=True, axi...  37.8 us
    all_gather x1, blocking collectives, per_device(): rates = lax.all_gather(conductive_number, 'wall', axis=1, tiled=True)  10.4 us
    all_to_all x1, starting transfers between devices, exchange(): lax.all_to_all(blocks, AXES, split_axis=0, concat_axis=0, tiled=True, axi...  7.1 us
    unnamed x15, local copies, waits for them, and re-layouts  7.1 us
    pallas_call x1, Pallas kernels, with_kernels(): pl.pallas_call(functools.partial(x_kernel, walls), in_specs=[pl.BlockSpec...  4.15 us
    pallas_call x1, Pallas kernels, with_kernels(): pl.pallas_call(y_forward_kernel, in_specs=[ANY] * 3, out_specs=[ANY, VMEM...  4.01 us
    pallas_call x1, Pallas kernels, with_kernels(): pl.pallas_call(functools.partial(y_inverse_kernel, 1.0 / (length * lines...  2.67 us
  transfers between devices with their start and end apart: 1, of which 1 were waited for; matrix products, arithmetic and copies ran while one was open for 0% of the time, Pallas kernels for 0%

profile of v2, /device:TPU:1, one launch (start us, length us, event | category | flops | bytes accessed | tf_op | source)
XLA Modules:
  0.0 125.0 jit_solution(1593729607140907781)
XLA Ops:
  0.0 0.0 copy-start.3
  0.0 1.6 %copy-done.3 = f32[2,4,64,1024]{3,2,1,0:T(8,128)S(1)} copy-done((f32[2,4,64,1024]{3,2,1,0:T(8,128)S(1)}, f32[2,4,64,1024]{3,2,1,0:T(8,128)}, u32[]{:S(2)}) %copy-start.3) | copy-done | bytes 2097176
  1.6 0.0 copy-start.4
  1.6 1.2 copy-done.4
  2.8 0.0 copy-start.5
  2.8 1.0 copy-done.5
  3.9 4.0 %y_forward.1 = (f32[32,2,32,256]{3,2,1,0:T(8,128)S(1)}, bf16[2,2,256,256]{3,2,1,0:T(8,128)(2,1)S(1)}, bf16[2,512,512]{2,1,0:T(8,128)(2,1)S(1)}) custom-call(f32[2,4,64,1024]{3,2,1,0:T(8,128)S(1)} %copy-done.3, bf16[2,2,256,256]{3,2,1,0:T(8,128)(2,1)S(1)} %copy-done.5, bf16[2,512,512]{2,1,0:T(8,128)(2,1)S(1)} %copy-done.4), custom_call_target="tpu_custom_call" | custom-call | flops 1207959552 | bytes 4194304 | tf_op jit(solution)/shard_map/y_forward/pallas_call | solution.py:257
  7.9 0.0 copy-start
  7.9 1.3 %copy-done = f32[32,2,32,256]{3,2,1,0:T(8,128)} copy-done((f32[32,2,32,256]{3,2,1,0:T(8,128)}, f32[32,2,32,256]{3,2,1,0:T(8,128)S(1)}, u32[]{:S(2)}) %copy-start) | copy-done | bytes 2097176
  9.2 0.0 copy-start.1
  9.2 0.8 copy-done.1
  10.0 0.0 copy-start.6
  10.0 7.1 %all-to-all-start = ((f32[32,2,32,256]{3,2,1,0:T(8,128)}), f32[32,2,32,256]{3,2,1,0:T(8,128)S(1)}, u32[]{:S(2)}, u32[]{:S(2)}) async-start(f32[32,2,32,256]{3,2,1,0:T(8,128)} %copy-done), calls=%async_computation | async-start | bytes 4194304 | tf_op jit(solution)/shard_map/all_to_all | solution.py:301
  17.1 0.0 copy-done.6
  17.1 10.4 %all-gather = f32[2,4,2]{1,2,0:T(2,128)S(1)} all-gather(f32[1,4,2]{1,2,0:T(2,128)S(1)} %bitcast.7), channel_id=1, replica_groups=mesh['wall'=2,'row'=16] {'wall'}, dimensions={0}, use_global_device_ids=true | all-gather | bytes 96 | tf_op jit(solution)/shard_map/all_gather | solution.py:359
  27.5 0.1 reshape.126
  27.6 37.8 %all-to-all-done.received_ref = f32[32,2,32,256]{3,2,1,0:T(8,128)S(1)} async-done(((f32[32,2,32,256]{3,2,1,0:T(8,128)}), f32[32,2,32,256]{3,2,1,0:T(8,128)S(1)}, u32[]{:S(2)}, u32[]{:S(2)}) %all-to-all-start) | async-done | bytes 2097184 | tf_op jit(solution)/shard_map/all_to_all | solution.py:301
  65.4 0.0 copy-start.2
  65.4 1.0 copy-done.2
  66.4 4.1 %x_filter.1 = f32[32,2,32,256]{3,2,1,0:T(8,128)S(1)} custom-call(f32[2,8]{1,0:T(2,128)S(1)} %bitcast.6, f32[32,1]{1,0:T(8,128)S(1)} %fusion.2.square_y_ref, f32[1,1024]{1,0:T(1,128)S(1)} %fusion.11.square_x_ref, bf16[2,2,256,256]{3,2,1,0:T(8,128)(2,1)S(1)} %copy-done.2, bf16[2,512,512]{2,1,0:T(8,128)(2,1)S(1)} %get-tuple-element.9.odd_ref, ...), custom_call_target="tpu_custom_call" | custom-call | flops 2415919104 | bytes 4194304 | tf_op jit(solution)/shard_map/x_filter/pallas_call | solution.py:273
  70.6 51.8 %all_to_all.10.spectrum_ref = f32[32,2,32,256]{3,2,1,0:T(8,128)S(1)} all-to-all(f32[32,2,32,256]{3,2,1,0:T(8,128)S(1)} %x_filter.1), channel_id=1, replica_groups={{0,4,8,12,1,5,9,13,2,6,10,14,3,7,11,15,16,20,24,28,17,21,25,29,18,22,26..., dimensions={0} | all-to-all | bytes 4194304 | tf_op jit(solution)/shard_map/all_to_all | solution.py:301
  122.4 2.7 %y_inverse.1 = f32[2,4,64,1024]{3,2,1,0:T(8,128)} custom-call(bf16[2,2,256,256]{3,2,1,0:T(8,128)(2,1)S(1)} %copy-done.2, bf16[2,512,512]{2,1,0:T(8,128)(2,1)S(1)} %get-tuple-element.9.odd_ref, f32[32,2,32,256]{3,2,1,0:T(8,128)S(1)} %all_to_all.10.spectrum_ref), custom_call_target="tpu_custom_call" | custom-call | flops 1207959552 | bytes 4194304 | tf_op jit(solution)/shard_map/y_inverse/pallas_call | solution.py:283
  (3 shorter events, 0.0 us)
Async XLA Ops:
  0.0 1.6 %copy-start.3 = (f32[2,4,64,1024]{3,2,1,0:T(8,128)S(1)}, f32[2,4,64,1024]{3,2,1,0:T(8,128)}, u32[]{:S(2)}) copy-start(f32[2,4,64,1024]{3,2,1,0:T(8,128)} %field_hbm.1) | copy-start | bytes 6291460
  1.6 1.2 copy-start.4
  2.8 1.0 copy-start.5
  7.9 1.3 %copy-start = (f32[32,2,32,256]{3,2,1,0:T(8,128)}, f32[32,2,32,256]{3,2,1,0:T(8,128)S(1)}, u32[]{:S(2)}) copy-start(f32[32,2,32,256]{3,2,1,0:T(8,128)S(1)} %get-tuple-element.10) | copy-start | bytes 6291460
  9.2 0.8 copy-start.1
  10.0 7.1 %copy-start.6 = (f32[2,4]{1,0:T(2,128)S(1)}, f32[2,4]{1,0:T(2,128)}, u32[]{:S(2)}) copy-start(f32[2,4]{1,0:T(2,128)} %param.5) | copy-start | bytes 100
  10.0 55.4 %all-to-all-start = ((f32[32,2,32,256]{3,2,1,0:T(8,128)}), f32[32,2,32,256]{3,2,1,0:T(8,128)S(1)}, u32[]{:S(2)}, u32[]{:S(2)}) async-start(f32[32,2,32,256]{3,2,1,0:T(8,128)} %copy-done), calls=%async_computation | async-start | bytes 4194304 | tf_op jit(solution)/shard_map/all_to_all | solution.py:301
  65.4 1.0 copy-start.2

commit v3 on v2

--- a/solution.py
+++ b/solution.py
@@ -12,7 +12,8 @@
 STEPS = 3
 AXES = ("wall", "row")
 LEVELS = 4
-VMEM_BYTES = 40 * 1024 * 1024
+MIB = 1024 * 1024
+TABLE_BYTES = 13 * MIB
 
 
 def wave_order(place, length):
@@ -63,8 +64,29 @@
 NT = ((1,), (1,))
 
 
-def part_tables(even_ref, odd_ref):
-    return [(even_ref[p, 0], even_ref[p, 1]) for p in range(2)] + [(odd_ref[0], odd_ref[1])]
+def stacked(tables, rows):
+    even, odd = tables
+    top = np.concatenate([even[0], even[1]], axis=2)
+    rest = np.zeros((2, rows - top.shape[1] - odd.shape[1], odd.shape[2]), odd.dtype)
+    return np.concatenate([top, odd, rest], axis=1)
+
+
+def part_tables(table_ref):
+    quarter = table_ref.shape[2] // 2
+    places = (
+        (slice(0, quarter), slice(0, quarter)),
+        (slice(0, quarter), slice(quarter, 2 * quarter)),
+        (slice(quarter, 3 * quarter), slice(0, 2 * quarter)),
+    )
+    return [(table_ref[0, rows, columns], table_ref[1, rows, columns]) for rows, columns in places]
+
+
+def table_loads(table_hbm, table_ref, sem):
+    quarter = table_ref.shape[2] // 2
+    return [
+        pltpu.make_async_copy(table_hbm.at[:, rows], table_ref.at[:, rows], sem.at[i])
+        for i, rows in enumerate((pl.ds(0, quarter), pl.ds(quarter, 2 * quarter)))
+    ]
 
 
 def part_ranges(total):
@@ -77,17 +99,16 @@
 
 
 def y_forward_kernel(
-    field_hbm, even_hbm, odd_hbm, out_hbm, even_ref, odd_ref, field_ref, out_ref, in_sem, table_sem,
-    out_sem,
+    field_hbm, table_hbm, out_hbm, field_ref, table_ref, out_ref, in_sem, table_sem, out_sem
 ):
     scalars, planes, lines, length = field_ref.shape
     rows = planes * lines
     quarter = length // 4
+    ranges = part_ranges(out_ref.shape[0])
     loads = [
         pltpu.make_async_copy(field_hbm.at[s], field_ref.at[s], in_sem.at[s]) for s in range(scalars)
     ]
-    even_load = pltpu.make_async_copy(even_hbm, even_ref, table_sem.at[0])
-    odd_load = pltpu.make_async_copy(odd_hbm, odd_ref, table_sem.at[1])
+    even_load, odd_load = table_loads(table_hbm, table_ref, table_sem)
     loads[0].start()
     even_load.start()
     odd_load.start()
@@ -96,19 +117,17 @@
     stores = []
     for s in range(scalars):
         loads[s].wait()
-        lines_of = [
+        first, second, third, fourth = fold([
             field_ref[s, :, :, q * quarter : (q + 1) * quarter].reshape(rows, quarter) for q in range(4)
-        ]
-        first, second, third, fourth = fold(lines_of)
-        parts = [first, second, jnp.concatenate([third, fourth], axis=1)]
-        for p, (low, high) in enumerate(part_ranges(out_ref.shape[0])):
+        ])
+        parts = [split(v) for v in (first, second, jnp.concatenate([third, fourth], axis=1))]
+        for p in (0, 1, 2) if s == 0 else (2, 0, 1):
             if s == 0 and p == 0:
                 even_load.wait()
             if s == 0 and p == 2:
                 odd_load.wait()
-            table = (odd_ref[0], odd_ref[1]) if p == 2 else (even_ref[p, 0], even_ref[p, 1])
-            waves = product(table, split(parts[p]), NT)
-            out_ref[low:high, s] = waves.reshape(high - low, -1, rows)
+            low, high = ranges[p]
+            out_ref[low:high, s] = product(part_tables(table_ref)[p], parts[p], NT).reshape(high - low, -1, rows)
             store = pltpu.make_async_copy(
                 out_ref.at[pl.ds(low, high - low), s],
                 out_hbm.at[pl.ds(low, high - low), s],
@@ -120,21 +139,34 @@
         store.wait()
 
 
-def y_inverse_kernel(norm, even_ref, odd_ref, spectrum_ref, out_hbm, out_ref, out_sem):
+def y_inverse_kernel(
+    norm, spectrum_ref, table_hbm, out_hbm, table_ref, out_ref, table_sem, out_sem
+):
     devices, scalars, waves, rows = spectrum_ref.shape
     planes, lines, length = out_ref.shape[1:]
     quarter = length // 4
-    tables = part_tables(even_ref, odd_ref)
+    even_load, odd_load = table_loads(table_hbm, table_ref, table_sem)
+    even_load.start()
+    odd_load.start()
+    turned = [
+        [
+            split((spectrum_ref[low:high, s].reshape(-1, rows) * norm).T)
+            for low, high in part_ranges(devices)
+        ]
+        for s in range(scalars)
+    ]
+    even_load.wait()
+    odd_load.wait()
     stores = []
     for s in range(scalars):
         first, second, third = (
-            product(split(spectrum_ref[low:high, s].reshape(-1, rows).T), table, NN)
-            for table, (low, high) in zip(tables, part_ranges(devices))
+            product(part, table, NN) for part, table in zip(turned[s], part_tables(table_ref))
         )
-        quarters = unfold(first * norm, second * norm, third[:, :quarter] * norm, third[:, quarter:] * norm)
-        for q, value in enumerate(quarters):
-            out_ref[s, :, :, q * quarter : (q + 1) * quarter] = value.reshape(planes, lines, quarter)
         for z in range(planes):
+            own = slice(z * lines, (z + 1) * lines)
+            quarters = unfold(first[own], second[own], third[own, :quarter], third[own, quarter:])
+            for q, value in enumerate(quarters):
+                out_ref[s, z, :, q * quarter : (q + 1) * quarter] = value
             store = pltpu.make_async_copy(out_ref.at[s, z], out_hbm.at[s, z], out_sem.at[s, z])
             store.start()
             stores.append(store)
@@ -143,8 +175,12 @@
 
 
 def x_kernel(
-    walls, rate_ref, square_y_ref, square_x_ref, even_ref, odd_ref, received_ref, out_ref, *line_refs
+    walls, rate_ref, square_y_ref, square_x_ref, received_ref, table_hbm, out_ref, table_ref,
+    table_sem, *line_refs
 ):
+    even_load, odd_load = table_loads(table_hbm, table_ref, table_sem)
+    even_load.start()
+    odd_load.start()
     devices, scalars, waves, rows = received_ref.shape
     groups = devices // walls
     length = line_refs[0].shape[1]
@@ -153,7 +189,6 @@
     planes = rows // lines
     count = walls * planes
     lower = lax.broadcasted_iota(jnp.int32, (waves, 128), 1) < lines
-    tables = part_tables(even_ref, odd_ref)
     ranges = part_ranges(length)
 
     def paired(a, b):
@@ -167,7 +202,7 @@
             for p in range(planes // 2):
                 yield w, slice(128 * p, 128 * (p + 1)), (w * planes + 2 * p) * waves
 
-    def forward(s):
+    def arrange(s):
         line_ref = line_refs[s]
         for w, lanes, top in tiles():
             for i in range(groups // 8):
@@ -183,7 +218,10 @@
                     columns = slice(quarter * q + 128 * i, quarter * q + 128 * (i + 1))
                     line_ref[top : top + waves, columns] = a
                     line_ref[top + waves : top + 2 * waves, columns] = b
-        for table, (low, high) in zip(tables, ranges):
+
+    def forward(s):
+        line_ref = line_refs[s]
+        for table, (low, high) in zip(part_tables(table_ref), ranges):
             line_ref[:, low:high] = product(split(line_ref[:, low:high]), table, NT)
 
     def diffuse(s):
@@ -213,11 +251,15 @@
     def inverse(s):
         line_ref = line_refs[s]
         first, second, third = (
-            product(split(line_ref[:, low:high]), table, NN) for table, (low, high) in zip(tables, ranges)
+            product(split(line_ref[:, low:high]), table, NN)
+            for table, (low, high) in zip(part_tables(table_ref), ranges)
         )
         quarters = unfold(first, second, third[:, :quarter], third[:, quarter:])
         for q, value in enumerate(quarters):
             line_ref[:, q * quarter : (q + 1) * quarter] = value
+
+    def send(s):
+        line_ref = line_refs[s]
         for w, lanes, top in tiles():
             for j in range(groups // 2):
                 columns = slice(128 * j, 128 * (j + 1))
@@ -228,12 +270,21 @@
                 out_ref[slot(w, 2 * j, groups), s, :, lanes] = a
                 out_ref[slot(w, 2 * j + 1, groups), s, :, lanes] = b
 
-    for phase in (forward, diffuse, inverse):
-        for s in range(scalars):
-            phase(s)
-
-
-PARAMS = pltpu.CompilerParams(vmem_limit_bytes=VMEM_BYTES)
+    for s in range(scalars):
+        arrange(s)
+    even_load.wait()
+    odd_load.wait()
+    phases = (forward, diffuse, inverse, send)
+    for time in range(len(phases) + scalars - 1):
+        for s in reversed(range(scalars)):
+            if 0 <= time - s < len(phases):
+                phases[time - s](s)
+
+
+def grant(mebibytes):
+    return pltpu.CompilerParams(vmem_limit_bytes=mebibytes * MIB)
+
+
 VMEM = pl.BlockSpec(memory_space=pltpu.VMEM)
 ANY = pl.BlockSpec(memory_space=pl.ANY)
 
@@ -248,51 +299,58 @@
     devices = walls * groups
     waves = length // devices
     rows = planes * lines
-    even, odd = tables
     blocks = jax.ShapeDtypeStruct((devices, scalars, waves, rows), jnp.float32)
-    shapes = [jax.ShapeDtypeStruct(t.shape, jnp.bfloat16) for t in tables]
     total = 8 * scalars * rows * length
     work = 9 * scalars * rows * length * length // 8
-
-    spectrum, even, odd = pl.pallas_call(
+    table = stacked(tables, TABLE_BYTES // (2 * length))
+    table_scratch = pltpu.VMEM((2, 3 * length // 4, length // 2), jnp.bfloat16)
+
+    spectrum = pl.pallas_call(
         y_forward_kernel,
-        in_specs=[ANY] * 3,
-        out_specs=[ANY, VMEM, VMEM],
-        out_shape=[blocks, *shapes],
+        in_specs=[ANY] * 2,
+        out_specs=ANY,
+        out_shape=blocks,
         scratch_shapes=[
             pltpu.VMEM(fields.shape, jnp.float32),
+            table_scratch,
             pltpu.VMEM(blocks.shape, jnp.float32),
             pltpu.SemaphoreType.DMA((scalars,)),
             pltpu.SemaphoreType.DMA((2,)),
             pltpu.SemaphoreType.DMA((scalars, 3)),
         ],
-        compiler_params=PARAMS,
+        compiler_params=grant(60),
         cost_estimate=cost(work, total),
         name="y_forward",
-    )(fields, even, odd)
+    )(fields, table)
     filtered = pl.pallas_call(
         functools.partial(x_kernel, walls),
-        in_specs=[pl.BlockSpec(memory_space=pltpu.SMEM)] + [VMEM] * 5,
+        in_specs=[pl.BlockSpec(memory_space=pltpu.SMEM)] + [VMEM] * 3 + [ANY],
         out_specs=VMEM,
         out_shape=blocks,
-        scratch_shapes=[pltpu.VMEM((walls * planes * waves, lines * groups), jnp.float32)] * scalars,
-        compiler_params=PARAMS,
+        scratch_shapes=[
+            table_scratch,
+            pltpu.SemaphoreType.DMA((2,)),
+            *[pltpu.VMEM((walls * planes * waves, lines * groups), jnp.float32)] * scalars,
+        ],
+        compiler_params=grant(48),
         cost_estimate=cost(2 * work, total),
         name="x_filter",
-    )(rates, square_y, square_x, even, odd, exchange(spectrum))
+    )(rates, square_y, square_x, exchange(spectrum), table)
     return pl.pallas_call(
         functools.partial(y_inverse_kernel, 1.0 / (length * lines * groups)),
-        in_specs=[VMEM] * 3,
+        in_specs=[VMEM, ANY],
         out_specs=ANY,
         out_shape=jax.ShapeDtypeStruct(fields.shape, jnp.float32),
         scratch_shapes=[
+            table_scratch,
             pltpu.VMEM(fields.shape, jnp.float32),
+            pltpu.SemaphoreType.DMA((2,)),
             pltpu.SemaphoreType.DMA((scalars, planes)),
         ],
-        compiler_params=PARAMS,
+        compiler_params=grant(48),
         cost_estimate=cost(work, total),
         name="y_inverse",
-    )(even, odd, exchange(filtered))
+    )(exchange(filtered), table)
 
 
 def exchange(blocks):

time: 125 us -> 123 us (0.984)
  local copies, waits for them, and re-layouts: 7.1 us -> 0.09 us
  Pallas kernels: 10.8 us -> 15.4 us
    unnamed x15 -> x3, local copies, waits for them, and re-layouts: 7.1 us -> 0.09 us
    pallas_call x1, Pallas kernels: 4.15 us -> 6.07 us  [with_kernels(): pl.pallas_call(functools.partial(x_kernel, walls), in_specs=[pl.BlockSpec...]
    pallas_call x1, Pallas kernels: 2.67 us -> 4.33 us  [with_kernels(): pl.pallas_call(functools.partial(y_inverse_kernel, 1.0 / (length * lines...]
where the time goes in v3:
time: 123 us
  blocking collectives  62.2 us (51%)
  waiting for transfers between devices  37.8 us (31%)
  Pallas kernels  15.4 us (13%)
  starting transfers between devices  7.11 us (6%)
    all_to_all x1, blocking collectives, exchange(): lax.all_to_all(blocks, AXES, split_axis=0, concat_axis=0, tiled=True, axi...  51.8 us
    all_to_all x1, waiting for transfers between devices, exchange(): lax.all_to_all(blocks, AXES, split_axis=0, concat_axis=0, tiled=True, axi...  37.8 us
    all_gather x1, blocking collectives, per_device(): rates = lax.all_gather(conductive_number, 'wall', axis=1, tiled=True)  10.4 us
    all_to_all x1, starting transfers between devices, exchange(): lax.all_to_all(blocks, AXES, split_axis=0, concat_axis=0, tiled=True, axi...  7.11 us
    pallas_call x1, Pallas kernels, with_kernels(): pl.pallas_call(functools.partial(x_kernel, walls), in_specs=[pl.BlockSpec...  6.07 us
    pallas_call x1, Pallas kernels, with_kernels(): pl.pallas_call(y_forward_kernel, in_specs=[ANY] * 2, out_specs=ANY, out_s...  4.97 us
    pallas_call x1, Pallas kernels, with_kernels(): pl.pallas_call(functools.partial(y_inverse_kernel, 1.0 / (length * lines...  4.33 us
  transfers between devices with their start and end apart: 1, of which 1 were waited for; matrix products, arithmetic and copies ran while one was open for 0% of the time, Pallas kernels for 0%

profile of v3, /device:TPU:1, one launch (start us, length us, event | category | flops | bytes accessed | tf_op | source)
XLA Modules:
  0.0 122.6 jit_solution(14281347802312145986)
XLA Ops:
  0.0 5.0 %y_forward.1 = f32[32,2,32,256]{3,2,1,0:T(8,128)} custom-call(f32[2,4,64,1024]{3,2,1,0:T(8,128)} %field_hbm.1, bf16[2,6656,512]{2,1,0:T(8,128)(2,1)} %constant.65.clone.table_hbm), custom_call_target="tpu_custom_call" | custom-call | flops 1207959552 | bytes 4194304 | tf_op jit(solution)/shard_map/y_forward/pallas_call | solution.py:308
  5.0 0.0 copy-start
  5.0 7.1 %all-to-all-start = ((f32[32,2,32,256]{3,2,1,0:T(8,128)}), f32[32,2,32,256]{3,2,1,0:T(8,128)S(1)}, u32[]{:S(2)}, u32[]{:S(2)}) async-start(f32[32,2,32,256]{3,2,1,0:T(8,128)} %y_forward.1), calls=%async_computation | async-start | bytes 4194304 | tf_op jit(solution)/shard_map/all_to_all | solution.py:359
  12.1 0.0 copy-done
  12.1 10.4 %all-gather = f32[2,4,2]{1,2,0:T(2,128)S(1)} all-gather(f32[1,4,2]{1,2,0:T(2,128)S(1)} %bitcast.7), channel_id=1, replica_groups=mesh['wall'=2,'row'=16] {'wall'}, dimensions={0}, use_global_device_ids=true | all-gather | bytes 96 | tf_op jit(solution)/shard_map/all_gather | solution.py:417
  22.5 0.1 reshape.126
  22.6 37.8 %all-to-all-done.received_ref = f32[32,2,32,256]{3,2,1,0:T(8,128)S(1)} async-done(((f32[32,2,32,256]{3,2,1,0:T(8,128)}), f32[32,2,32,256]{3,2,1,0:T(8,128)S(1)}, u32[]{:S(2)}, u32[]{:S(2)}) %all-to-all-start) | async-done | bytes 2097184 | tf_op jit(solution)/shard_map/all_to_all | solution.py:359
  60.4 6.1 %x_filter.1 = f32[32,2,32,256]{3,2,1,0:T(8,128)S(1)} custom-call(f32[2,8]{1,0:T(2,128)S(1)} %bitcast.6, f32[32,1]{1,0:T(8,128)S(1)} %fusion.2.square_y_ref, f32[1,1024]{1,0:T(1,128)S(1)} %fusion.11.square_x_ref, f32[32,2,32,256]{3,2,1,0:T(8,128)S(1)} %all-to-all-done.received_ref, bf16[2,6656,512]{2,1,0:T(8,128)(2,1)} %constant.65.clone.table_hbm), custom_call_target="tpu_custom_call" | custom-call | flops 2415919104 | bytes 4194304 | tf_op jit(solution)/shard_map/x_filter/pallas_call | solution.py:325
  66.4 51.8 %all_to_all.10.spectrum_ref = f32[32,2,32,256]{3,2,1,0:T(8,128)S(1)} all-to-all(f32[32,2,32,256]{3,2,1,0:T(8,128)S(1)} %x_filter.1), channel_id=1, replica_groups={{0,4,8,12,1,5,9,13,2,6,10,14,3,7,11,15,16,20,24,28,17,21,25,29,18,22,26..., dimensions={0} | all-to-all | bytes 4194304 | tf_op jit(solution)/shard_map/all_to_all | solution.py:359
  118.2 4.3 %y_inverse.1 = f32[2,4,64,1024]{3,2,1,0:T(8,128)} custom-call(f32[32,2,32,256]{3,2,1,0:T(8,128)S(1)} %all_to_all.10.spectrum_ref, bf16[2,6656,512]{2,1,0:T(8,128)(2,1)} %constant.65.clone.table_hbm), custom_call_target="tpu_custom_call" | custom-call | flops 1207959552 | bytes 4194304 | tf_op jit(solution)/shard_map/y_inverse/pallas_call | solution.py:339
  (3 shorter events, 0.0 us)
Async XLA Ops:
  5.0 7.1 %copy-start = (f32[2,4]{1,0:T(2,128)S(1)}, f32[2,4]{1,0:T(2,128)}, u32[]{:S(2)}) copy-start(f32[2,4]{1,0:T(2,128)} %param.4) | copy-start | bytes 100
  5.0 55.4 %all-to-all-start = ((f32[32,2,32,256]{3,2,1,0:T(8,128)}), f32[32,2,32,256]{3,2,1,0:T(8,128)S(1)}, u32[]{:S(2)}, u32[]{:S(2)}) async-start(f32[32,2,32,256]{3,2,1,0:T(8,128)} %y_forward.1), calls=%async_computation | async-start | bytes 4194304 | tf_op jit(solution)/shard_map/all_to_all | solution.py:359

commit v4 on v3

--- a/solution.py
+++ b/solution.py
@@ -139,34 +139,28 @@
         store.wait()
 
 
-def y_inverse_kernel(
-    norm, spectrum_ref, table_hbm, out_hbm, table_ref, out_ref, table_sem, out_sem
-):
+def hold_kernel(after_hbm, table_hbm, table_ref, sem):
+    del after_hbm
+    load = pltpu.make_async_copy(table_hbm.at[:, pl.ds(0, table_ref.shape[1])], table_ref, sem.at[0])
+    load.start()
+    load.wait()
+
+
+def y_inverse_kernel(norm, table_ref, spectrum_ref, out_hbm, out_ref, out_sem):
     devices, scalars, waves, rows = spectrum_ref.shape
     planes, lines, length = out_ref.shape[1:]
     quarter = length // 4
-    even_load, odd_load = table_loads(table_hbm, table_ref, table_sem)
-    even_load.start()
-    odd_load.start()
-    turned = [
-        [
-            split((spectrum_ref[low:high, s].reshape(-1, rows) * norm).T)
-            for low, high in part_ranges(devices)
-        ]
-        for s in range(scalars)
-    ]
-    even_load.wait()
-    odd_load.wait()
+    tables = part_tables(table_ref)
     stores = []
     for s in range(scalars):
         first, second, third = (
-            product(part, table, NN) for part, table in zip(turned[s], part_tables(table_ref))
+            product(split(spectrum_ref[low:high, s].reshape(-1, rows).T), table, NN)
+            for table, (low, high) in zip(tables, part_ranges(devices))
         )
+        quarters = unfold(first * norm, second * norm, third[:, :quarter] * norm, third[:, quarter:] * norm)
+        for q, value in enumerate(quarters):
+            out_ref[s, :, :, q * quarter : (q + 1) * quarter] = value.reshape(planes, lines, quarter)
         for z in range(planes):
-            own = slice(z * lines, (z + 1) * lines)
-            quarters = unfold(first[own], second[own], third[own, :quarter], third[own, quarter:])
-            for q, value in enumerate(quarters):
-                out_ref[s, z, :, q * quarter : (q + 1) * quarter] = value
             store = pltpu.make_async_copy(out_ref.at[s, z], out_hbm.at[s, z], out_sem.at[s, z])
             store.start()
             stores.append(store)
@@ -175,12 +169,8 @@
 
 
 def x_kernel(
-    walls, rate_ref, square_y_ref, square_x_ref, received_ref, table_hbm, out_ref, table_ref,
-    table_sem, *line_refs
+    walls, rate_ref, square_y_ref, square_x_ref, table_ref, received_ref, out_ref, *line_refs
 ):
-    even_load, odd_load = table_loads(table_hbm, table_ref, table_sem)
-    even_load.start()
-    odd_load.start()
     devices, scalars, waves, rows = received_ref.shape
     groups = devices // walls
     length = line_refs[0].shape[1]
@@ -189,6 +179,7 @@
     planes = rows // lines
     count = walls * planes
     lower = lax.broadcasted_iota(jnp.int32, (waves, 128), 1) < lines
+    tables = part_tables(table_ref)
     ranges = part_ranges(length)
 
     def paired(a, b):
@@ -202,7 +193,7 @@
             for p in range(planes // 2):
                 yield w, slice(128 * p, 128 * (p + 1)), (w * planes + 2 * p) * waves
 
-    def arrange(s):
+    def forward(s):
         line_ref = line_refs[s]
         for w, lanes, top in tiles():
             for i in range(groups // 8):
@@ -218,10 +209,7 @@
                     columns = slice(quarter * q + 128 * i, quarter * q + 128 * (i + 1))
                     line_ref[top : top + waves, columns] = a
                     line_ref[top + waves : top + 2 * waves, columns] = b
-
-    def forward(s):
-        line_ref = line_refs[s]
-        for table, (low, high) in zip(part_tables(table_ref), ranges):
+        for table, (low, high) in zip(tables, ranges):
             line_ref[:, low:high] = product(split(line_ref[:, low:high]), table, NT)
 
     def diffuse(s):
@@ -251,15 +239,11 @@
     def inverse(s):
         line_ref = line_refs[s]
         first, second, third = (
-            product(split(line_ref[:, low:high]), table, NN)
-            for table, (low, high) in zip(part_tables(table_ref), ranges)
+            product(split(line_ref[:, low:high]), table, NN) for table, (low, high) in zip(tables, ranges)
         )
         quarters = unfold(first, second, third[:, :quarter], third[:, quarter:])
         for q, value in enumerate(quarters):
             line_ref[:, q * quarter : (q + 1) * quarter] = value
-
-    def send(s):
-        line_ref = line_refs[s]
         for w, lanes, top in tiles():
             for j in range(groups // 2):
                 columns = slice(128 * j, 128 * (j + 1))
@@ -270,15 +254,9 @@
                 out_ref[slot(w, 2 * j, groups), s, :, lanes] = a
                 out_ref[slot(w, 2 * j + 1, groups), s, :, lanes] = b
 
-    for s in range(scalars):
-        arrange(s)
-    even_load.wait()
-    odd_load.wait()
-    phases = (forward, diffuse, inverse, send)
-    for time in range(len(phases) + scalars - 1):
-        for s in reversed(range(scalars)):
-            if 0 <= time - s < len(phases):
-                phases[time - s](s)
+    for phase in (forward, diffuse, inverse):
+        for s in range(scalars):
+            phase(s)
 
 
 def grant(mebibytes):
@@ -303,7 +281,7 @@
     total = 8 * scalars * rows * length
     work = 9 * scalars * rows * length * length // 8
     table = stacked(tables, TABLE_BYTES // (2 * length))
-    table_scratch = pltpu.VMEM((2, 3 * length // 4, length // 2), jnp.bfloat16)
+    table_shape = (2, 3 * length // 4, length // 2)
 
     spectrum = pl.pallas_call(
         y_forward_kernel,
@@ -312,7 +290,7 @@
         out_shape=blocks,
         scratch_shapes=[
             pltpu.VMEM(fields.shape, jnp.float32),
-            table_scratch,
+            pltpu.VMEM(table_shape, jnp.bfloat16),
             pltpu.VMEM(blocks.shape, jnp.float32),
             pltpu.SemaphoreType.DMA((scalars,)),
             pltpu.SemaphoreType.DMA((2,)),
@@ -322,35 +300,39 @@
         cost_estimate=cost(work, total),
         name="y_forward",
     )(fields, table)
+    held = pl.pallas_call(
+        hold_kernel,
+        in_specs=[ANY] * 2,
+        out_specs=VMEM,
+        out_shape=jax.ShapeDtypeStruct(table_shape, jnp.bfloat16),
+        scratch_shapes=[pltpu.SemaphoreType.DMA((1,))],
+        compiler_params=grant(48),
+        cost_estimate=cost(0, 2 * MIB),
+        name="hold",
+    )(spectrum[0, 0, :8, :128], table)
     filtered = pl.pallas_call(
         functools.partial(x_kernel, walls),
-        in_specs=[pl.BlockSpec(memory_space=pltpu.SMEM)] + [VMEM] * 3 + [ANY],
+        in_specs=[pl.BlockSpec(memory_space=pltpu.SMEM)] + [VMEM] * 4,
         out_specs=VMEM,
         out_shape=blocks,
-        scratch_shapes=[
-            table_scratch,
-            pltpu.SemaphoreType.DMA((2,)),
-            *[pltpu.VMEM((walls * planes * waves, lines * groups), jnp.float32)] * scalars,
-        ],
-        compiler_params=grant(48),
+        scratch_shapes=[pltpu.VMEM((walls * planes * waves, lines * groups), jnp.float32)] * scalars,
+        compiler_params=grant(40),
         cost_estimate=cost(2 * work, total),
         name="x_filter",
-    )(rates, square_y, square_x, exchange(spectrum), table)
+    )(rates, square_y, square_x, held, exchange(spectrum))
     return pl.pallas_call(
         functools.partial(y_inverse_kernel, 1.0 / (length * lines * groups)),
-        in_specs=[VMEM, ANY],
+        in_specs=[VMEM] * 2,
         out_specs=ANY,
         out_shape=jax.ShapeDtypeStruct(fields.shape, jnp.float32),
         scratch_shapes=[
-            table_scratch,
             pltpu.VMEM(fields.shape, jnp.float32),
-            pltpu.SemaphoreType.DMA((2,)),
             pltpu.SemaphoreType.DMA((scalars, planes)),
         ],
-        compiler_params=grant(48),
+        compiler_params=grant(40),
         cost_estimate=cost(work, total),
         name="y_inverse",
-    )(exchange(filtered), table)
+    )(held, exchange(filtered))
 
 
 def exchange(blocks):

time: 123 us -> 120 us (0.976)
  waiting for transfers between devices: 37.8 us -> 35.6 us
    all_to_all x1, waiting for transfers between devices: 37.8 us -> 35.6 us  [exchange(): lax.all_to_all(blocks, AXES, split_axis=0, concat_axis=0, tiled=True, axi...]
    pallas_call x1, Pallas kernels: 4.33 us -> 2.68 us  [with_kernels(): pl.pallas_call(functools.partial(y_inverse_kernel, 1.0 / (length * lines...]
    pallas_call x0 -> x1, Pallas kernels: none -> 1.42 us  [with_kernels(): pl.pallas_call(hold_kernel, in_specs=[ANY] * 2, out_specs=VMEM, out_shape...]
  transfers between devices with their start and end apart: 1 -> 1, of which waited for: 1 -> 1; matrix products, arithmetic and copies ran while one was open for 0% -> 1% of each run, Pallas kernels for 0% -> 1%
where the time goes in v4:
time: 120 us
  blocking collectives  62.2 us (52%)
  waiting for transfers between devices  35.6 us (30%)
  Pallas kernels  14.3 us (12%)
  starting transfers between devices  7.16 us (6%)
    all_to_all x1, blocking collectives, exchange(): lax.all_to_all(blocks, AXES, split_axis=0, concat_axis=0, tiled=True, axi...  51.8 us
    all_to_all x1, waiting for transfers between devices, exchange(): lax.all_to_all(blocks, AXES, split_axis=0, concat_axis=0, tiled=True, axi...  35.6 us
    all_gather x1, blocking collectives, per_device(): rates = lax.all_gather(conductive_number, 'wall', axis=1, tiled=True)  10.4 us
    all_to_all x1, starting transfers between devices, exchange(): lax.all_to_all(blocks, AXES, split_axis=0, concat_axis=0, tiled=True, axi...  7.16 us
    pallas_call x1, Pallas kernels, with_kernels(): pl.pallas_call(functools.partial(x_kernel, walls), in_specs=[pl.BlockSpec...  5.2 us
    pallas_call x1, Pallas kernels, with_kernels(): pl.pallas_call(y_forward_kernel, in_specs=[ANY] * 2, out_specs=ANY, out_s...  4.97 us
    pallas_call x1, Pallas kernels, with_kernels(): pl.pallas_call(functools.partial(y_inverse_kernel, 1.0 / (length * lines...  2.68 us
  transfers between devices with their start and end apart: 1, of which 1 were waited for; matrix products, arithmetic and copies ran while one was open for 1% of the time, Pallas kernels for 1%

profile of v4, /device:TPU:1, one launch (start us, length us, event | category | flops | bytes accessed | tf_op | source)
XLA Modules:
  0.0 120.1 jit_solution(16915424702098692358)
XLA Ops:
  0.0 5.0 %y_forward.1 = f32[32,2,32,256]{3,2,1,0:T(8,128)} custom-call(f32[2,4,64,1024]{3,2,1,0:T(8,128)} %field_hbm.1, bf16[2,6656,512]{2,1,0:T(8,128)(2,1)} %constant.65.clone.table_hbm), custom_call_target="tpu_custom_call" | custom-call | flops 1207959552 | bytes 4194304 | tf_op jit(solution)/shard_map/y_forward/pallas_call | solution.py:286
  5.0 0.0 copy-start
  5.0 7.2 %all-to-all-start = ((f32[32,2,32,256]{3,2,1,0:T(8,128)}), f32[32,2,32,256]{3,2,1,0:T(8,128)}, u32[]{:S(2)}, u32[]{:S(2)}) async-start(f32[32,2,32,256]{3,2,1,0:T(8,128)} %y_forward.1), calls=%async_computation | async-start | bytes 4194304 | tf_op jit(solution)/shard_map/all_to_all | solution.py:341
  12.2 0.0 copy-done
  12.2 10.4 %all-gather = f32[2,4,2]{1,2,0:T(2,128)S(1)} all-gather(f32[1,4,2]{1,2,0:T(2,128)S(1)} %bitcast.9), channel_id=1, replica_groups=mesh['wall'=2,'row'=16] {'wall'}, dimensions={0}, use_global_device_ids=true | all-gather | bytes 96 | tf_op jit(solution)/shard_map/all_gather | solution.py:399
  22.6 0.1 reshape.126
  22.7 0.7 slice_bitcast_fusion.after_hbm
  23.4 1.4 %hold.1.table_ref = bf16[2,768,512]{2,1,0:T(8,128)(2,1)S(1)} custom-call(f32[8,128]{1,0:T(8,128)S(1)} %slice_bitcast_fusion.after_hbm, bf16[2,6656,512]{2,1,0:T(8,128)(2,1)} %constant.65.clone.table_hbm), custom_call_target="tpu_custom_call" | custom-call | bytes 2097152 | tf_op jit(solution)/shard_map/hold/pallas_call | solution.py:303
  24.8 35.6 %all-to-all-done.received_ref = f32[32,2,32,256]{3,2,1,0:T(8,128)} async-done(((f32[32,2,32,256]{3,2,1,0:T(8,128)}), f32[32,2,32,256]{3,2,1,0:T(8,128)}, u32[]{:S(2)}, u32[]{:S(2)}) %all-to-all-start) | async-done | bytes 2097184 | tf_op jit(solution)/shard_map/all_to_all | solution.py:341
  60.5 5.2 %x_filter.1 = f32[32,2,32,256]{3,2,1,0:T(8,128)S(1)} custom-call(f32[2,8]{1,0:T(2,128)S(1)} %bitcast.8, f32[32,1]{1,0:T(8,128)S(1)} %fusion.2.square_y_ref, f32[1,1024]{1,0:T(1,128)S(1)} %fusion.11.square_x_ref, bf16[2,768,512]{2,1,0:T(8,128)(2,1)S(1)} %hold.1.table_ref, f32[32,2,32,256]{3,2,1,0:T(8,128)} %all-to-all-done.received_ref), custom_call_target="tpu_custom_call" | custom-call | flops 2415919104 | bytes 4194304 | tf_op jit(solution)/shard_map/x_filter/pallas_call | solution.py:313
  65.7 51.8 %all_to_all.10.spectrum_ref = f32[32,2,32,256]{3,2,1,0:T(8,128)S(1)} all-to-all(f32[32,2,32,256]{3,2,1,0:T(8,128)S(1)} %x_filter.1), channel_id=1, replica_groups={{0,4,8,12,1,5,9,13,2,6,10,14,3,7,11,15,16,20,24,28,17,21,25,29,18,22,26..., dimensions={0} | all-to-all | bytes 4194304 | tf_op jit(solution)/shard_map/all_to_all | solution.py:341
  117.5 2.7 %y_inverse.1 = f32[2,4,64,1024]{3,2,1,0:T(8,128)} custom-call(bf16[2,768,512]{2,1,0:T(8,128)(2,1)S(1)} %hold.1.table_ref, f32[32,2,32,256]{3,2,1,0:T(8,128)S(1)} %all_to_all.10.spectrum_ref), custom_call_target="tpu_custom_call" | custom-call | flops 1207959552 | bytes 4194304 | tf_op jit(solution)/shard_map/y_inverse/pallas_call | solution.py:323
  (3 shorter events, 0.0 us)
Async XLA Ops:
  5.0 7.2 %copy-start = (f32[2,4]{1,0:T(2,128)S(1)}, f32[2,4]{1,0:T(2,128)}, u32[]{:S(2)}) copy-start(f32[2,4]{1,0:T(2,128)} %param.4) | copy-start | bytes 100
  5.0 55.5 %all-to-all-start = ((f32[32,2,32,256]{3,2,1,0:T(8,128)}), f32[32,2,32,256]{3,2,1,0:T(8,128)}, u32[]{:S(2)}, u32[]{:S(2)}) async-start(f32[32,2,32,256]{3,2,1,0:T(8,128)} %y_forward.1), calls=%async_computation | async-start | bytes 4194304 | tf_op jit(solution)/shard_map/all_to_all | solution.py:341

commit v5 on v4

--- a/solution.py
+++ b/solution.py
@@ -10,6 +10,7 @@
 from jax.sharding import PartitionSpec as P
 
 STEPS = 3
+HEIGHT = 16
 AXES = ("wall", "row")
 LEVELS = 4
 MIB = 1024 * 1024
@@ -105,22 +106,31 @@
     rows = planes * lines
     quarter = length // 4
     ranges = part_ranges(out_ref.shape[0])
+    halves = [pl.ds(0, planes // 2), pl.ds(planes // 2, planes // 2)]
     loads = [
-        pltpu.make_async_copy(field_hbm.at[s], field_ref.at[s], in_sem.at[s]) for s in range(scalars)
+        [
+            pltpu.make_async_copy(field_hbm.at[s, h], field_ref.at[s, h], in_sem.at[s, i])
+            for i, h in enumerate(halves)
+        ]
+        for s in range(scalars)
     ]
     even_load, odd_load = table_loads(table_hbm, table_ref, table_sem)
-    loads[0].start()
-    even_load.start()
-    odd_load.start()
-    for load in loads[1:]:
+    for load in (*loads[0], even_load, odd_load, *sum(loads[1:], [])):
         load.start()
     stores = []
     for s in range(scalars):
-        loads[s].wait()
-        first, second, third, fourth = fold([
-            field_ref[s, :, :, q * quarter : (q + 1) * quarter].reshape(rows, quarter) for q in range(4)
-        ])
-        parts = [split(v) for v in (first, second, jnp.concatenate([third, fourth], axis=1))]
+        pieces = []
+        for load, h in zip(loads[s], halves):
+            load.wait()
+            first, second, third, fourth = fold([
+                field_ref[s, h, :, q * quarter : (q + 1) * quarter].reshape(rows // 2, quarter)
+                for q in range(4)
+            ])
+            folded = (first, second, jnp.concatenate([third, fourth], axis=1))
+            pieces.append([split(value) for value in folded])
+        parts = [
+            tuple(jnp.concatenate([piece[p][i] for piece in pieces]) for i in range(2)) for p in range(3)
+        ]
         for p in (0, 1, 2) if s == 0 else (2, 0, 1):
             if s == 0 and p == 0:
                 even_load.wait()
@@ -169,7 +179,8 @@
 
 
 def x_kernel(
-    walls, rate_ref, square_y_ref, square_x_ref, table_ref, received_ref, out_ref, *line_refs
+    walls, rate_ref, square_y_ref, square_x_ref, table_ref, received_hbm, out_ref, received_ref, sem,
+    *line_refs
 ):
     devices, scalars, waves, rows = received_ref.shape
     groups = devices // walls
@@ -179,6 +190,19 @@
     planes = rows // lines
     count = walls * planes
     lower = lax.broadcasted_iota(jnp.int32, (waves, 128), 1) < lines
+    loads = [
+        [
+            pltpu.make_async_copy(
+                received_hbm.at[pl.ds(w * groups, groups), s],
+                received_ref.at[pl.ds(w * groups, groups), s],
+                sem.at[s, w],
+            )
+            for w in range(walls)
+        ]
+        for s in range(scalars)
+    ]
+    for load in sum(loads, []):
+        load.start()
     tables = part_tables(table_ref)
     ranges = part_ranges(length)
 
@@ -196,6 +220,8 @@
     def forward(s):
         line_ref = line_refs[s]
         for w, lanes, top in tiles():
+            if lanes.start == 0:
+                loads[s][w].wait()
             for i in range(groups // 8):
                 left, right = (
                     fold([
@@ -215,26 +241,26 @@
     def diffuse(s):
         line_ref = line_refs[s]
         rates = [rate_ref[s, z] for z in range(count)]
-        damping_y = [jnp.exp(-rate * square_y_ref[...]) for rate in rates]
-        for j in range(length // 128):
-            columns = slice(128 * j, 128 * (j + 1))
-            square_x = square_x_ref[:, columns]
-            damping = [jnp.exp(-rate * square_x) * dy for rate, dy in zip(rates, damping_y)]
-            field = [line_ref[z * waves : (z + 1) * waves, columns] for z in range(count)]
-            for step in range(STEPS):
-                updated = []
-                for z in range(count):
-                    value = (1.0 - 2.0 * rates[z]) * field[z]
-                    if z == 0:
-                        around = field[1]
-                    elif z == count - 1:
-                        around = field[z - 1]
-                    else:
-                        around = field[z - 1] + field[z + 1]
-                    updated.append(damping[z] * (value + rates[z] * around))
-                field = updated
-            for z in range(count):
-                line_ref[z * waves : (z + 1) * waves, columns] = field[z]
+        damping_x = [jnp.exp(-rate * square_x_ref[...]) for rate in rates]
+        for i in range(waves // HEIGHT):
+            square_y = square_y_ref[HEIGHT * i : HEIGHT * (i + 1)]
+            damping_y = [jnp.exp(-rate * square_y) for rate in rates]
+            starts = [z * waves + HEIGHT * i for z in range(count)]
+            for j in range(length // 128):
+                columns = slice(128 * j, 128 * (j + 1))
+                damping = [dx[:, columns] * dy for dx, dy in zip(damping_x, damping_y)]
+                own = [d * (1.0 - 2.0 * rate) for d, rate in zip(damping, rates)]
+                around = [d * rate for d, rate in zip(damping, rates)]
+                field = [line_ref[top : top + HEIGHT, columns] for top in starts]
+                for step in range(STEPS):
+                    sums = [
+                        field[1],
+                        *[field[z - 1] + field[z + 1] for z in range(1, count - 1)],
+                        field[count - 2],
+                    ]
+                    field = [own[z] * field[z] + around[z] * sums[z] for z in range(count)]
+                for top, value in zip(starts, field):
+                    line_ref[top : top + HEIGHT, columns] = value
 
     def inverse(s):
         line_ref = line_refs[s]
@@ -292,7 +318,7 @@
             pltpu.VMEM(fields.shape, jnp.float32),
             pltpu.VMEM(table_shape, jnp.bfloat16),
             pltpu.VMEM(blocks.shape, jnp.float32),
-            pltpu.SemaphoreType.DMA((scalars,)),
+            pltpu.SemaphoreType.DMA((scalars, 2)),
             pltpu.SemaphoreType.DMA((2,)),
             pltpu.SemaphoreType.DMA((scalars, 3)),
         ],
@@ -312,10 +338,14 @@
     )(spectrum[0, 0, :8, :128], table)
     filtered = pl.pallas_call(
         functools.partial(x_kernel, walls),
-        in_specs=[pl.BlockSpec(memory_space=pltpu.SMEM)] + [VMEM] * 4,
+        in_specs=[pl.BlockSpec(memory_space=pltpu.SMEM)] + [VMEM] * 3 + [ANY],
         out_specs=VMEM,
         out_shape=blocks,
-        scratch_shapes=[pltpu.VMEM((walls * planes * waves, lines * groups), jnp.float32)] * scalars,
+        scratch_shapes=[
+            pltpu.VMEM(blocks.shape, jnp.float32),
+            pltpu.SemaphoreType.DMA((scalars, walls)),
+            *[pltpu.VMEM((walls * planes * waves, lines * groups), jnp.float32)] * scalars,
+        ],
         compiler_params=grant(40),
         cost_estimate=cost(2 * work, total),
         name="x_filter",
@@ -401,7 +431,7 @@
     place = own * waves + jnp.arange(waves, dtype=jnp.int32)
     square_y = signed_square(wave_order(place, length), length)[:, None]
     square_x = signed_square(wave_order(jnp.arange(length_x), length_x), length_x)[None, :]
-    fits = lines == 64 and planes % 2 == 0 and waves % 8 == 0 and groups % 8 == 0
+    fits = lines == 64 and planes % 2 == 0 and waves % HEIGHT == 0 and groups % 8 == 0
     if fits and length == length_x and walls * groups % 4 == 0:
         return with_kernels(thermal_scalars, rates, walls, square_y, square_x, tables_of(length))
     return with_arrays(

time: 120 us -> 121 us (level)
  no operation moved by 1% of the time
where the time goes in v5:
time: 121 us
  blocking collectives  62.2 us (51%)
  waiting for transfers between devices  35.6 us (29%)
  Pallas kernels  15.1 us (12%)
  starting transfers between devices  7.16 us (6%)
    all_to_all x1, blocking collectives, exchange(): lax.all_to_all(blocks, AXES, split_axis=0, concat_axis=0, tiled=True, axi...  51.8 us
    all_to_all x1, waiting for transfers between devices, exchange(): lax.all_to_all(blocks, AXES, split_axis=0, concat_axis=0, tiled=True, axi...  35.6 us
    all_gather x1, blocking collectives, per_device(): rates = lax.all_gather(conductive_number, 'wall', axis=1, tiled=True)  10.4 us
    all_to_all x1, starting transfers between devices, exchange(): lax.all_to_all(blocks, AXES, split_axis=0, concat_axis=0, tiled=True, axi...  7.16 us
    pallas_call x1, Pallas kernels, with_kernels(): pl.pallas_call(functools.partial(x_kernel, walls), in_specs=[pl.BlockSpec...  5.93 us
    pallas_call x1, Pallas kernels, with_kernels(): pl.pallas_call(y_forward_kernel, in_specs=[ANY] * 2, out_specs=ANY, out_s...  5.04 us
    pallas_call x1, Pallas kernels, with_kernels(): pl.pallas_call(functools.partial(y_inverse_kernel, 1.0 / (length * lines...  2.68 us
  transfers between devices with their start and end apart: 1, of which 1 were waited for; matrix products, arithmetic and copies ran while one was open for 1% of the time, Pallas kernels for 1%

profile of v5, /device:TPU:1, one launch (start us, length us, event | category | flops | bytes accessed | tf_op | source)
XLA Modules:
  0.0 120.9 jit_solution(7729185815144602085)
XLA Ops:
  0.0 5.0 %y_forward.1 = f32[32,2,32,256]{3,2,1,0:T(8,128)} custom-call(f32[2,4,64,1024]{3,2,1,0:T(8,128)} %field_hbm.1, bf16[2,6656,512]{2,1,0:T(8,128)(2,1)} %constant.65.clone.table_hbm), custom_call_target="tpu_custom_call" | custom-call | flops 1207959552 | bytes 4194304 | tf_op jit(solution)/shard_map/y_forward/pallas_call | solution.py:312
  5.0 0.0 copy-start
  5.1 7.2 %all-to-all-start = ((f32[32,2,32,256]{3,2,1,0:T(8,128)}), f32[32,2,32,256]{3,2,1,0:T(8,128)}, u32[]{:S(2)}, u32[]{:S(2)}) async-start(f32[32,2,32,256]{3,2,1,0:T(8,128)} %y_forward.1), calls=%async_computation | async-start | bytes 4194304 | tf_op jit(solution)/shard_map/all_to_all | solution.py:371
  12.2 0.0 copy-done
  12.2 10.4 %all-gather = f32[2,4,2]{1,2,0:T(2,128)S(1)} all-gather(f32[1,4,2]{1,2,0:T(2,128)S(1)} %bitcast.9), channel_id=1, replica_groups=mesh['wall'=2,'row'=16] {'wall'}, dimensions={0}, use_global_device_ids=true | all-gather | bytes 96 | tf_op jit(solution)/shard_map/all_gather | solution.py:429
  22.7 0.1 reshape.126
  22.7 0.7 slice_bitcast_fusion.after_hbm
  23.4 1.4 %hold.1.table_ref = bf16[2,768,512]{2,1,0:T(8,128)(2,1)S(1)} custom-call(f32[8,128]{1,0:T(8,128)S(1)} %slice_bitcast_fusion.after_hbm, bf16[2,6656,512]{2,1,0:T(8,128)(2,1)} %constant.65.clone.table_hbm), custom_call_target="tpu_custom_call" | custom-call | bytes 2097152 | tf_op jit(solution)/shard_map/hold/pallas_call | solution.py:329
  24.9 35.6 %all-to-all-done.received_hbm = f32[32,2,32,256]{3,2,1,0:T(8,128)} async-done(((f32[32,2,32,256]{3,2,1,0:T(8,128)}), f32[32,2,32,256]{3,2,1,0:T(8,128)}, u32[]{:S(2)}, u32[]{:S(2)}) %all-to-all-start) | async-done | bytes 2097184 | tf_op jit(solution)/shard_map/all_to_all | solution.py:371
  60.5 5.9 %x_filter.1 = f32[32,2,32,256]{3,2,1,0:T(8,128)S(1)} custom-call(f32[2,8]{1,0:T(2,128)S(1)} %bitcast.8, f32[32,1]{1,0:T(8,128)S(1)} %fusion.2.square_y_ref, f32[1,1024]{1,0:T(1,128)S(1)} %fusion.11.square_x_ref, bf16[2,768,512]{2,1,0:T(8,128)(2,1)S(1)} %hold.1.table_ref, f32[32,2,32,256]{3,2,1,0:T(8,128)} %all-to-all-done.received_hbm), custom_call_target="tpu_custom_call" | custom-call | flops 2415919104 | bytes 4194304 | tf_op jit(solution)/shard_map/x_filter/pallas_call | solution.py:339
  66.5 51.8 %all_to_all.10.spectrum_ref = f32[32,2,32,256]{3,2,1,0:T(8,128)S(1)} all-to-all(f32[32,2,32,256]{3,2,1,0:T(8,128)S(1)} %x_filter.1), channel_id=1, replica_groups={{0,4,8,12,1,5,9,13,2,6,10,14,3,7,11,15,16,20,24,28,17,21,25,29,18,22,26..., dimensions={0} | all-to-all | bytes 4194304 | tf_op jit(solution)/shard_map/all_to_all | solution.py:371
  118.3 2.7 %y_inverse.1 = f32[2,4,64,1024]{3,2,1,0:T(8,128)} custom-call(bf16[2,768,512]{2,1,0:T(8,128)(2,1)S(1)} %hold.1.table_ref, f32[32,2,32,256]{3,2,1,0:T(8,128)S(1)} %all_to_all.10.spectrum_ref), custom_call_target="tpu_custom_call" | custom-call | flops 1207959552 | bytes 4194304 | tf_op jit(solution)/shard_map/y_inverse/pallas_call | solution.py:353
  (3 shorter events, 0.0 us)
Async XLA Ops:
  5.0 7.2 %copy-start = (f32[2,4]{1,0:T(2,128)S(1)}, f32[2,4]{1,0:T(2,128)}, u32[]{:S(2)}) copy-start(f32[2,4]{1,0:T(2,128)} %param.4) | copy-start | bytes 100
  5.1 55.5 %all-to-all-start = ((f32[32,2,32,256]{3,2,1,0:T(8,128)}), f32[32,2,32,256]{3,2,1,0:T(8,128)}, u32[]{:S(2)}, u32[]{:S(2)}) async-start(f32[32,2,32,256]{3,2,1,0:T(8,128)} %y_forward.1), calls=%async_computation | async-start | bytes 4194304 | tf_op jit(solution)/shard_map/all_to_all | solution.py:371

commit v6 on v4

--- a/solution.py
+++ b/solution.py
@@ -13,7 +13,7 @@
 AXES = ("wall", "row")
 LEVELS = 4
 MIB = 1024 * 1024
-TABLE_BYTES = 13 * MIB
+TABLE_BYTES = 21 * MIB
 
 
 def wave_order(place, length):
@@ -306,7 +306,7 @@
         out_specs=VMEM,
         out_shape=jax.ShapeDtypeStruct(table_shape, jnp.bfloat16),
         scratch_shapes=[pltpu.SemaphoreType.DMA((1,))],
-        compiler_params=grant(48),
+        compiler_params=grant(40),
         cost_estimate=cost(0, 2 * MIB),
         name="hold",
     )(spectrum[0, 0, :8, :128], table)

time: 120 us -> 120 us (level)
  no operation moved by 1% of the time
where the time goes in v6:
time: 120 us
  blocking collectives  62.2 us (52%)
  waiting for transfers between devices  35.6 us (30%)
  Pallas kernels  14.3 us (12%)
  starting transfers between devices  7.16 us (6%)
    all_to_all x1, blocking collectives, exchange(): lax.all_to_all(blocks, AXES, split_axis=0, concat_axis=0, tiled=True, axi...  51.8 us
    all_to_all x1, waiting for transfers between devices, exchange(): lax.all_to_all(blocks, AXES, split_axis=0, concat_axis=0, tiled=True, axi...  35.6 us
    all_gather x1, blocking collectives, per_device(): rates = lax.all_gather(conductive_number, 'wall', axis=1, tiled=True)  10.4 us
    all_to_all x1, starting transfers between devices, exchange(): lax.all_to_all(blocks, AXES, split_axis=0, concat_axis=0, tiled=True, axi...  7.16 us
    pallas_call x1, Pallas kernels, with_kernels(): pl.pallas_call(functools.partial(x_kernel, walls), in_specs=[pl.BlockSpec...  5.2 us
    pallas_call x1, Pallas kernels, with_kernels(): pl.pallas_call(y_forward_kernel, in_specs=[ANY] * 2, out_specs=ANY, out_s...  4.97 us
    pallas_call x1, Pallas kernels, with_kernels(): pl.pallas_call(functools.partial(y_inverse_kernel, 1.0 / (length * lines...  2.68 us
  transfers between devices with their start and end apart: 1, of which 1 were waited for; matrix products, arithmetic and copies ran while one was open for 1% of the time, Pallas kernels for 1%

profile of v6, /device:TPU:1, one launch (start us, length us, event | category | flops | bytes accessed | tf_op | source)
XLA Modules:
  0.0 120.1 jit_solution(7647505588392220795)
XLA Ops:
  0.0 5.0 %y_forward.1 = f32[32,2,32,256]{3,2,1,0:T(8,128)} custom-call(f32[2,4,64,1024]{3,2,1,0:T(8,128)} %field_hbm.1, bf16[2,10752,512]{2,1,0:T(8,128)(2,1)} %constant.65.clone.table_hbm), custom_call_target="tpu_custom_call" | custom-call | flops 1207959552 | bytes 4194304 | tf_op jit(solution)/shard_map/y_forward/pallas_call | solution.py:286
  5.0 0.0 copy-start
  5.0 7.2 %all-to-all-start = ((f32[32,2,32,256]{3,2,1,0:T(8,128)}), f32[32,2,32,256]{3,2,1,0:T(8,128)}, u32[]{:S(2)}, u32[]{:S(2)}) async-start(f32[32,2,32,256]{3,2,1,0:T(8,128)} %y_forward.1), calls=%async_computation | async-start | bytes 4194304 | tf_op jit(solution)/shard_map/all_to_all | solution.py:341
  12.2 0.0 copy-done
  12.2 10.4 %all-gather = f32[2,4,2]{1,2,0:T(2,128)S(1)} all-gather(f32[1,4,2]{1,2,0:T(2,128)S(1)} %bitcast.9), channel_id=1, replica_groups=mesh['wall'=2,'row'=16] {'wall'}, dimensions={0}, use_global_device_ids=true | all-gather | bytes 96 | tf_op jit(solution)/shard_map/all_gather | solution.py:399
  22.6 0.1 reshape.126
  22.7 0.7 slice_bitcast_fusion.after_hbm
  23.4 1.4 %hold.1.table_ref = bf16[2,768,512]{2,1,0:T(8,128)(2,1)S(1)} custom-call(f32[8,128]{1,0:T(8,128)S(1)} %slice_bitcast_fusion.after_hbm, bf16[2,10752,512]{2,1,0:T(8,128)(2,1)} %constant.65.clone.table_hbm), custom_call_target="tpu_custom_call" | custom-call | bytes 2097152 | tf_op jit(solution)/shard_map/hold/pallas_call | solution.py:303
  24.8 35.6 %all-to-all-done.received_ref = f32[32,2,32,256]{3,2,1,0:T(8,128)} async-done(((f32[32,2,32,256]{3,2,1,0:T(8,128)}), f32[32,2,32,256]{3,2,1,0:T(8,128)}, u32[]{:S(2)}, u32[]{:S(2)}) %all-to-all-start) | async-done | bytes 2097184 | tf_op jit(solution)/shard_map/all_to_all | solution.py:341
  60.5 5.2 %x_filter.1 = f32[32,2,32,256]{3,2,1,0:T(8,128)S(1)} custom-call(f32[2,8]{1,0:T(2,128)S(1)} %bitcast.8, f32[32,1]{1,0:T(8,128)S(1)} %fusion.2.square_y_ref, f32[1,1024]{1,0:T(1,128)S(1)} %fusion.11.square_x_ref, bf16[2,768,512]{2,1,0:T(8,128)(2,1)S(1)} %hold.1.table_ref, f32[32,2,32,256]{3,2,1,0:T(8,128)} %all-to-all-done.received_ref), custom_call_target="tpu_custom_call" | custom-call | flops 2415919104 | bytes 4194304 | tf_op jit(solution)/shard_map/x_filter/pallas_call | solution.py:313
  65.7 51.8 %all_to_all.10.spectrum_ref = f32[32,2,32,256]{3,2,1,0:T(8,128)S(1)} all-to-all(f32[32,2,32,256]{3,2,1,0:T(8,128)S(1)} %x_filter.1), channel_id=1, replica_groups={{0,4,8,12,1,5,9,13,2,6,10,14,3,7,11,15,16,20,24,28,17,21,25,29,18,22,26..., dimensions={0} | all-to-all | bytes 4194304 | tf_op jit(solution)/shard_map/all_to_all | solution.py:341
  117.5 2.7 %y_inverse.1 = f32[2,4,64,1024]{3,2,1,0:T(8,128)} custom-call(bf16[2,768,512]{2,1,0:T(8,128)(2,1)S(1)} %hold.1.table_ref, f32[32,2,32,256]{3,2,1,0:T(8,128)S(1)} %all_to_all.10.spectrum_ref), custom_call_target="tpu_custom_call" | custom-call | flops 1207959552 | bytes 4194304 | tf_op jit(solution)/shard_map/y_inverse/pallas_call | solution.py:323
  (3 shorter events, 0.0 us)
Async XLA Ops:
  5.0 7.2 %copy-start = (f32[2,4]{1,0:T(2,128)S(1)}, f32[2,4]{1,0:T(2,128)}, u32[]{:S(2)}) copy-start(f32[2,4]{1,0:T(2,128)} %param.4) | copy-start | bytes 100
  5.0 55.5 %all-to-all-start = ((f32[32,2,32,256]{3,2,1,0:T(8,128)}), f32[32,2,32,256]{3,2,1,0:T(8,128)}, u32[]{:S(2)}, u32[]{:S(2)}) async-start(f32[32,2,32,256]{3,2,1,0:T(8,128)} %y_forward.1), calls=%async_computation | async-start | bytes 4194304 | tf_op jit(solution)/shard_map/all_to_all | solution.py:341

commit v7 on v6

--- a/solution.py
+++ b/solution.py
@@ -13,7 +13,6 @@
 AXES = ("wall", "row")
 LEVELS = 4
 MIB = 1024 * 1024
-TABLE_BYTES = 21 * MIB
 
 
 def wave_order(place, length):
@@ -64,11 +63,9 @@
 NT = ((1,), (1,))
 
 
-def stacked(tables, rows):
+def stacked(tables):
     even, odd = tables
-    top = np.concatenate([even[0], even[1]], axis=2)
-    rest = np.zeros((2, rows - top.shape[1] - odd.shape[1], odd.shape[2]), odd.dtype)
-    return np.concatenate([top, odd, rest], axis=1)
+    return np.concatenate([np.concatenate([even[0], even[1]], axis=2), odd], axis=1)
 
 
 def part_tables(table_ref):
@@ -99,7 +96,7 @@
 
 
 def y_forward_kernel(
-    field_hbm, table_hbm, out_hbm, field_ref, table_ref, out_ref, in_sem, table_sem, out_sem
+    field_hbm, table_hbm, out_hbm, table_ref, field_ref, out_ref, in_sem, table_sem, out_sem
 ):
     scalars, planes, lines, length = field_ref.shape
     rows = planes * lines
@@ -139,13 +136,6 @@
         store.wait()
 
 
-def hold_kernel(after_hbm, table_hbm, table_ref, sem):
-    del after_hbm
-    load = pltpu.make_async_copy(table_hbm.at[:, pl.ds(0, table_ref.shape[1])], table_ref, sem.at[0])
-    load.start()
-    load.wait()
-
-
 def y_inverse_kernel(norm, table_ref, spectrum_ref, out_hbm, out_ref, out_sem):
     devices, scalars, waves, rows = spectrum_ref.shape
     planes, lines, length = out_ref.shape[1:]
@@ -260,7 +250,7 @@
 
 
 def grant(mebibytes):
-    return pltpu.CompilerParams(vmem_limit_bytes=mebibytes * MIB)
+    return pltpu.CompilerParams(vmem_limit_bytes=int(mebibytes * MIB))
 
 
 VMEM = pl.BlockSpec(memory_space=pltpu.VMEM)
@@ -280,36 +270,24 @@
     blocks = jax.ShapeDtypeStruct((devices, scalars, waves, rows), jnp.float32)
     total = 8 * scalars * rows * length
     work = 9 * scalars * rows * length * length // 8
-    table = stacked(tables, TABLE_BYTES // (2 * length))
-    table_shape = (2, 3 * length // 4, length // 2)
-
-    spectrum = pl.pallas_call(
+    table = stacked(tables)
+
+    spectrum, table = pl.pallas_call(
         y_forward_kernel,
         in_specs=[ANY] * 2,
-        out_specs=ANY,
-        out_shape=blocks,
+        out_specs=[ANY, VMEM],
+        out_shape=[blocks, jax.ShapeDtypeStruct(table.shape, jnp.bfloat16)],
         scratch_shapes=[
             pltpu.VMEM(fields.shape, jnp.float32),
-            pltpu.VMEM(table_shape, jnp.bfloat16),
             pltpu.VMEM(blocks.shape, jnp.float32),
             pltpu.SemaphoreType.DMA((scalars,)),
             pltpu.SemaphoreType.DMA((2,)),
             pltpu.SemaphoreType.DMA((scalars, 3)),
         ],
-        compiler_params=grant(60),
+        compiler_params=grant(51.5),
         cost_estimate=cost(work, total),
         name="y_forward",
     )(fields, table)
-    held = pl.pallas_call(
-        hold_kernel,
-        in_specs=[ANY] * 2,
-        out_specs=VMEM,
-        out_shape=jax.ShapeDtypeStruct(table_shape, jnp.bfloat16),
-        scratch_shapes=[pltpu.SemaphoreType.DMA((1,))],
-        compiler_params=grant(40),
-        cost_estimate=cost(0, 2 * MIB),
-        name="hold",
-    )(spectrum[0, 0, :8, :128], table)
     filtered = pl.pallas_call(
         functools.partial(x_kernel, walls),
         in_specs=[pl.BlockSpec(memory_space=pltpu.SMEM)] + [VMEM] * 4,
@@ -319,7 +297,7 @@
         compiler_params=grant(40),
         cost_estimate=cost(2 * work, total),
         name="x_filter",
-    )(rates, square_y, square_x, held, exchange(spectrum))
+    )(rates, square_y, square_x, table, exchange(spectrum))
     return pl.pallas_call(
         functools.partial(y_inverse_kernel, 1.0 / (length * lines * groups)),
         in_specs=[VMEM] * 2,
@@ -332,7 +310,7 @@
         compiler_params=grant(40),
         cost_estimate=cost(work, total),
         name="y_inverse",
-    )(held, exchange(filtered))
+    )(table, exchange(filtered))
 
 
 def exchange(blocks):

time: 120 us -> 122 us (1.017)
  Pallas kernels: 14.3 us -> 11.8 us
  waiting for transfers between devices: 35.6 us -> 37.8 us
  local copies, waits for them, and re-layouts: 0.78 us -> 2.65 us
    unnamed x3 -> x7, local copies, waits for them, and re-layouts: 0.09 us -> 2.65 us
    all_to_all x1, waiting for transfers between devices: 35.6 us -> 37.8 us  [exchange(): lax.all_to_all(blocks, AXES, split_axis=0, concat_axis=0, tiled=True, axi...]
    pallas_call x2 -> x1, Pallas kernels: 6.38 us -> 4.97 us  [with_kernels(): pl.pallas_call(y_forward_kernel, in_specs=[ANY] * 2, out_specs=[ANY, VMEM...]
  transfers between devices with their start and end apart: 1 -> 1, of which waited for: 1 -> 1; matrix products, arithmetic and copies ran while one was open for 1% -> 0% of each run, Pallas kernels for 1% -> 0%
where the time goes in v7:
time: 122 us
  blocking collectives  62.2 us (51%)
  waiting for transfers between devices  37.8 us (31%)
  Pallas kernels  11.8 us (10%)
  starting transfers between devices  7.1 us (6%)
  local copies, waits for them, and re-layouts  2.65 us (2%)
    all_to_all x1, blocking collectives, exchange(): lax.all_to_all(blocks, AXES, split_axis=0, concat_axis=0, tiled=True, axi...  51.8 us
    all_to_all x1, waiting for transfers between devices, exchange(): lax.all_to_all(blocks, AXES, split_axis=0, concat_axis=0, tiled=True, axi...  37.8 us
    all_gather x1, blocking collectives, per_device(): rates = lax.all_gather(conductive_number, 'wall', axis=1, tiled=True)  10.4 us
    all_to_all x1, starting transfers between devices, exchange(): lax.all_to_all(blocks, AXES, split_axis=0, concat_axis=0, tiled=True, axi...  7.1 us
    pallas_call x1, Pallas kernels, with_kernels(): pl.pallas_call(y_forward_kernel, in_specs=[ANY] * 2, out_specs=[ANY, VMEM...  4.97 us
    pallas_call x1, Pallas kernels, with_kernels(): pl.pallas_call(functools.partial(x_kernel, walls), in_specs=[pl.BlockSpec...  4.16 us
    pallas_call x1, Pallas kernels, with_kernels(): pl.pallas_call(functools.partial(y_inverse_kernel, 1.0 / (length * lines...  2.68 us
    unnamed x7, local copies, waits for them, and re-layouts  2.65 us
  transfers between devices with their start and end apart: 1, of which 1 were waited for; matrix products, arithmetic and copies ran while one was open for 0% of the time, Pallas kernels for 0%

profile of v7, /device:TPU:1, one launch (start us, length us, event | category | flops | bytes accessed | tf_op | source)
XLA Modules:
  0.0 121.6 jit_solution(3244114239752073710)
XLA Ops:
  0.0 5.0 %y_forward.1 = (f32[32,2,32,256]{3,2,1,0:T(8,128)}, bf16[2,768,512]{2,1,0:T(8,128)(2,1)S(1)}) custom-call(f32[2,4,64,1024]{3,2,1,0:T(8,128)} %field_hbm.1, bf16[2,768,512]{2,1,0:T(8,128)(2,1)} %constant.65.clone.table_hbm), custom_call_target="tpu_custom_call" | custom-call | flops 1207959552 | bytes 4194304 | tf_op jit(solution)/shard_map/y_forward/pallas_call | solution.py:275
  5.0 0.0 copy-start
  5.0 1.1 copy-done
  6.1 0.0 copy-start.2
  6.1 7.1 %all-to-all-start = ((f32[32,2,32,256]{3,2,1,0:T(8,128)}), f32[32,2,32,256]{3,2,1,0:T(8,128)S(1)}, u32[]{:S(2)}, u32[]{:S(2)}) async-start(f32[32,2,32,256]{3,2,1,0:T(8,128)} %get-tuple-element.8), calls=%async_computation | async-start | bytes 4194304 | tf_op jit(solution)/shard_map/all_to_all | solution.py:319
  13.2 0.0 copy-done.2
  13.3 10.4 %all-gather = f32[2,4,2]{1,2,0:T(2,128)S(1)} all-gather(f32[1,4,2]{1,2,0:T(2,128)S(1)} %bitcast.7), channel_id=1, replica_groups=mesh['wall'=2,'row'=16] {'wall'}, dimensions={0}, use_global_device_ids=true | all-gather | bytes 96 | tf_op jit(solution)/shard_map/all_gather | solution.py:377
  23.6 0.1 reshape.126
  23.8 37.8 %all-to-all-done.received_ref = f32[32,2,32,256]{3,2,1,0:T(8,128)S(1)} async-done(((f32[32,2,32,256]{3,2,1,0:T(8,128)}), f32[32,2,32,256]{3,2,1,0:T(8,128)S(1)}, u32[]{:S(2)}, u32[]{:S(2)}) %all-to-all-start) | async-done | bytes 2097184 | tf_op jit(solution)/shard_map/all_to_all | solution.py:319
  61.5 0.0 copy-start.1
  61.5 1.4 %copy-done.1 = bf16[2,768,512]{2,1,0:T(8,128)(2,1)S(1)} copy-done((bf16[2,768,512]{2,1,0:T(8,128)(2,1)S(1)}, bf16[2,768,512]{2,1,0:T(8,128)(2,1)}, u32[]{:S(2)}) %copy-start.1) | copy-done | bytes 1572888
  62.9 4.2 %x_filter.1 = f32[32,2,32,256]{3,2,1,0:T(8,128)S(1)} custom-call(f32[2,8]{1,0:T(2,128)S(1)} %bitcast.6, f32[32,1]{1,0:T(8,128)S(1)} %fusion.2.square_y_ref, f32[1,1024]{1,0:T(1,128)S(1)} %fusion.11.square_x_ref, bf16[2,768,512]{2,1,0:T(8,128)(2,1)S(1)} %copy-done.1, f32[32,2,32,256]{3,2,1,0:T(8,128)S(1)} %all-to-all-done.received_ref), custom_call_target="tpu_custom_call" | custom-call | flops 2415919104 | bytes 4194304 | tf_op jit(solution)/shard_map/x_filter/pallas_call | solution.py:291
  67.1 51.8 %all_to_all.10.spectrum_ref = f32[32,2,32,256]{3,2,1,0:T(8,128)S(1)} all-to-all(f32[32,2,32,256]{3,2,1,0:T(8,128)S(1)} %x_filter.1), channel_id=1, replica_groups={{0,4,8,12,1,5,9,13,2,6,10,14,3,7,11,15,16,20,24,28,17,21,25,29,18,22,26..., dimensions={0} | all-to-all | bytes 4194304 | tf_op jit(solution)/shard_map/all_to_all | solution.py:319
  118.9 2.7 %y_inverse.1 = f32[2,4,64,1024]{3,2,1,0:T(8,128)} custom-call(bf16[2,768,512]{2,1,0:T(8,128)(2,1)S(1)} %copy-done.1, f32[32,2,32,256]{3,2,1,0:T(8,128)S(1)} %all_to_all.10.spectrum_ref), custom_call_target="tpu_custom_call" | custom-call | flops 1207959552 | bytes 4194304 | tf_op jit(solution)/shard_map/y_inverse/pallas_call | solution.py:301
  (3 shorter events, 0.0 us)
Async XLA Ops:
  5.0 1.2 copy-start
  6.1 7.1 %copy-start.2 = (f32[2,4]{1,0:T(2,128)S(1)}, f32[2,4]{1,0:T(2,128)}, u32[]{:S(2)}) copy-start(f32[2,4]{1,0:T(2,128)} %param.4) | copy-start | bytes 100
  6.1 55.4 %all-to-all-start = ((f32[32,2,32,256]{3,2,1,0:T(8,128)}), f32[32,2,32,256]{3,2,1,0:T(8,128)S(1)}, u32[]{:S(2)}, u32[]{:S(2)}) async-start(f32[32,2,32,256]{3,2,1,0:T(8,128)} %get-tuple-element.8), calls=%async_computation | async-start | bytes 4194304 | tf_op jit(solution)/shard_map/all_to_all | solution.py:319
  61.5 1.4 %copy-start.1 = (bf16[2,768,512]{2,1,0:T(8,128)(2,1)S(1)}, bf16[2,768,512]{2,1,0:T(8,128)(2,1)}, u32[]{:S(2)}) copy-start(bf16[2,768,512]{2,1,0:T(8,128)(2,1)} %copy-done) | copy-start | bytes 4718596

commit v8 on v7

--- a/solution.py
+++ b/solution.py
@@ -13,6 +13,7 @@
 AXES = ("wall", "row")
 LEVELS = 4
 MIB = 1024 * 1024
+TABLE_BYTES = 13 * MIB
 
 
 def wave_order(place, length):
@@ -63,27 +64,27 @@
 NT = ((1,), (1,))
 
 
-def stacked(tables):
+def stacked(tables, rows):
     even, odd = tables
-    return np.concatenate([np.concatenate([even[0], even[1]], axis=2), odd], axis=1)
-
-
-def part_tables(table_ref):
-    quarter = table_ref.shape[2] // 2
-    places = (
-        (slice(0, quarter), slice(0, quarter)),
-        (slice(0, quarter), slice(quarter, 2 * quarter)),
-        (slice(quarter, 3 * quarter), slice(0, 2 * quarter)),
-    )
-    return [(table_ref[0, rows, columns], table_ref[1, rows, columns]) for rows, columns in places]
-
-
-def table_loads(table_hbm, table_ref, sem):
-    quarter = table_ref.shape[2] // 2
-    return [
-        pltpu.make_async_copy(table_hbm.at[:, rows], table_ref.at[:, rows], sem.at[i])
-        for i, rows in enumerate((pl.ds(0, quarter), pl.ds(quarter, 2 * quarter)))
-    ]
+    top = np.concatenate([even[0], even[1]], axis=2)
+    rest = np.zeros((2, rows - top.shape[1] - odd.shape[1], odd.shape[2]), odd.dtype)
+    return np.concatenate([top, odd, rest], axis=1)
+
+
+def part_tables(even_ref, odd_ref):
+    quarter = even_ref.shape[1]
+    columns = (slice(0, quarter), slice(quarter, 2 * quarter))
+    return [(even_ref[0, :, c], even_ref[1, :, c]) for c in columns] + [(odd_ref[0], odd_ref[1])]
+
+
+def even_copy(table_hbm, even_ref, sem):
+    rows = pl.ds(0, even_ref.shape[1])
+    return pltpu.make_async_copy(table_hbm.at[:, rows], even_ref, sem)
+
+
+def odd_copy(table_hbm, odd_ref, sem):
+    rows = pl.ds(odd_ref.shape[1] // 2, odd_ref.shape[1])
+    return pltpu.make_async_copy(table_hbm.at[:, rows], odd_ref, sem)
 
 
 def part_ranges(total):
@@ -96,7 +97,7 @@
 
 
 def y_forward_kernel(
-    field_hbm, table_hbm, out_hbm, table_ref, field_ref, out_ref, in_sem, table_sem, out_sem
+    field_hbm, table_hbm, out_hbm, odd_ref, field_ref, even_ref, out_ref, in_sem, table_sem, out_sem
 ):
     scalars, planes, lines, length = field_ref.shape
     rows = planes * lines
@@ -105,7 +106,8 @@
     loads = [
         pltpu.make_async_copy(field_hbm.at[s], field_ref.at[s], in_sem.at[s]) for s in range(scalars)
     ]
-    even_load, odd_load = table_loads(table_hbm, table_ref, table_sem)
+    even_load = even_copy(table_hbm, even_ref, table_sem.at[0])
+    odd_load = odd_copy(table_hbm, odd_ref, table_sem.at[1])
     loads[0].start()
     even_load.start()
     odd_load.start()
@@ -124,7 +126,7 @@
             if s == 0 and p == 2:
                 odd_load.wait()
             low, high = ranges[p]
-            out_ref[low:high, s] = product(part_tables(table_ref)[p], parts[p], NT).reshape(high - low, -1, rows)
+            out_ref[low:high, s] = product(part_tables(even_ref, odd_ref)[p], parts[p], NT).reshape(high - low, -1, rows)
             store = pltpu.make_async_copy(
                 out_ref.at[pl.ds(low, high - low), s],
                 out_hbm.at[pl.ds(low, high - low), s],
@@ -136,17 +138,25 @@
         store.wait()
 
 
-def y_inverse_kernel(norm, table_ref, spectrum_ref, out_hbm, out_ref, out_sem):
+def y_inverse_kernel(
+    norm, odd_ref, spectrum_ref, table_hbm, out_hbm, even_ref, out_ref, table_sem, out_sem
+):
+    even_load = even_copy(table_hbm, even_ref, table_sem.at[0])
+    even_load.start()
     devices, scalars, waves, rows = spectrum_ref.shape
     planes, lines, length = out_ref.shape[1:]
     quarter = length // 4
-    tables = part_tables(table_ref)
+    ranges = part_ranges(devices)
     stores = []
     for s in range(scalars):
-        first, second, third = (
-            product(split(spectrum_ref[low:high, s].reshape(-1, rows).T), table, NN)
-            for table, (low, high) in zip(tables, part_ranges(devices))
-        )
+        parts = {}
+        for p in (2, 0, 1):
+            low, high = ranges[p]
+            turned = split(spectrum_ref[low:high, s].reshape(-1, rows).T)
+            if s == 0 and p == 0:
+                even_load.wait()
+            parts[p] = product(turned, part_tables(even_ref, odd_ref)[p], NN)
+        first, second, third = (parts[p] for p in range(3))
         quarters = unfold(first * norm, second * norm, third[:, :quarter] * norm, third[:, quarter:] * norm)
         for q, value in enumerate(quarters):
             out_ref[s, :, :, q * quarter : (q + 1) * quarter] = value.reshape(planes, lines, quarter)
@@ -159,8 +169,11 @@
 
 
 def x_kernel(
-    walls, rate_ref, square_y_ref, square_x_ref, table_ref, received_ref, out_ref, *line_refs
+    walls, rate_ref, square_y_ref, square_x_ref, odd_ref, received_ref, table_hbm, out_ref, even_ref,
+    table_sem, *line_refs
 ):
+    even_load = even_copy(table_hbm, even_ref, table_sem.at[0])
+    even_load.start()
     devices, scalars, waves, rows = received_ref.shape
     groups = devices // walls
     length = line_refs[0].shape[1]
@@ -169,7 +182,6 @@
     planes = rows // lines
     count = walls * planes
     lower = lax.broadcasted_iota(jnp.int32, (waves, 128), 1) < lines
-    tables = part_tables(table_ref)
     ranges = part_ranges(length)
 
     def paired(a, b):
@@ -199,7 +211,11 @@
                     columns = slice(quarter * q + 128 * i, quarter * q + 128 * (i + 1))
                     line_ref[top : top + waves, columns] = a
                     line_ref[top + waves : top + 2 * waves, columns] = b
-        for table, (low, high) in zip(tables, ranges):
+        for p in (2, 0, 1):
+            low, high = ranges[p]
+            if s == 0 and p == 0:
+                even_load.wait()
+            table = part_tables(even_ref, odd_ref)[p]
             line_ref[:, low:high] = product(split(line_ref[:, low:high]), table, NT)
 
     def diffuse(s):
@@ -229,7 +245,8 @@
     def inverse(s):
         line_ref = line_refs[s]
         first, second, third = (
-            product(split(line_ref[:, low:high]), table, NN) for table, (low, high) in zip(tables, ranges)
+            product(split(line_ref[:, low:high]), table, NN)
+            for table, (low, high) in zip(part_tables(even_ref, odd_ref), ranges)
         )
         quarters = unfold(first, second, third[:, :quarter], third[:, quarter:])
         for q, value in enumerate(quarters):
@@ -270,47 +287,56 @@
     blocks = jax.ShapeDtypeStruct((devices, scalars, waves, rows), jnp.float32)
     total = 8 * scalars * rows * length
     work = 9 * scalars * rows * length * length // 8
-    table = stacked(tables)
-
-    spectrum, table = pl.pallas_call(
+    table = stacked(tables, TABLE_BYTES // (2 * length))
+    even_scratch = pltpu.VMEM((2, length // 4, length // 2), jnp.bfloat16)
+    odd_shape = jax.ShapeDtypeStruct((2, length // 2, length // 2), jnp.bfloat16)
+
+    spectrum, odd = pl.pallas_call(
         y_forward_kernel,
         in_specs=[ANY] * 2,
         out_specs=[ANY, VMEM],
-        out_shape=[blocks, jax.ShapeDtypeStruct(table.shape, jnp.bfloat16)],
+        out_shape=[blocks, odd_shape],
         scratch_shapes=[
             pltpu.VMEM(fields.shape, jnp.float32),
+            even_scratch,
             pltpu.VMEM(blocks.shape, jnp.float32),
             pltpu.SemaphoreType.DMA((scalars,)),
             pltpu.SemaphoreType.DMA((2,)),
             pltpu.SemaphoreType.DMA((scalars, 3)),
         ],
-        compiler_params=grant(51.5),
+        compiler_params=grant(52),
         cost_estimate=cost(work, total),
         name="y_forward",
     )(fields, table)
     filtered = pl.pallas_call(
         functools.partial(x_kernel, walls),
-        in_specs=[pl.BlockSpec(memory_space=pltpu.SMEM)] + [VMEM] * 4,
+        in_specs=[pl.BlockSpec(memory_space=pltpu.SMEM)] + [VMEM] * 4 + [ANY],
         out_specs=VMEM,
         out_shape=blocks,
-        scratch_shapes=[pltpu.VMEM((walls * planes * waves, lines * groups), jnp.float32)] * scalars,
-        compiler_params=grant(40),
+        scratch_shapes=[
+            even_scratch,
+            pltpu.SemaphoreType.DMA((1,)),
+            *[pltpu.VMEM((walls * planes * waves, lines * groups), jnp.float32)] * scalars,
+        ],
+        compiler_params=grant(48),
         cost_estimate=cost(2 * work, total),
         name="x_filter",
-    )(rates, square_y, square_x, table, exchange(spectrum))
+    )(rates, square_y, square_x, odd, exchange(spectrum), table)
     return pl.pallas_call(
         functools.partial(y_inverse_kernel, 1.0 / (length * lines * groups)),
-        in_specs=[VMEM] * 2,
+        in_specs=[VMEM] * 2 + [ANY],
         out_specs=ANY,
         out_shape=jax.ShapeDtypeStruct(fields.shape, jnp.float32),
         scratch_shapes=[
+            even_scratch,
             pltpu.VMEM(fields.shape, jnp.float32),
+            pltpu.SemaphoreType.DMA((1,)),
             pltpu.SemaphoreType.DMA((scalars, planes)),
         ],
-        compiler_params=grant(40),
+        compiler_params=grant(48),
         cost_estimate=cost(work, total),
         name="y_inverse",
-    )(table, exchange(filtered))
+    )(odd, exchange(filtered), table)
 
 
 def exchange(blocks):

time: 122 us -> 121 us (level)
  local copies, waits for them, and re-layouts: 2.65 us -> 0.09 us
  Pallas kernels: 11.8 us -> 13.1 us
    unnamed x7 -> x3, local copies, waits for them, and re-layouts: 2.65 us -> 0.09 us
where the time goes in v8:
time: 121 us; the launch traced here: 120 us
  blocking collectives  62.2 us (51%)
  waiting for transfers between devices  37.8 us (31%)
  Pallas kernels  13.1 us (11%)
  starting transfers between devices  7.11 us (6%)
    all_to_all x1, blocking collectives, exchange(): lax.all_to_all(blocks, AXES, split_axis=0, concat_axis=0, tiled=True, axi...  51.8 us
    all_to_all x1, waiting for transfers between devices, exchange(): lax.all_to_all(blocks, AXES, split_axis=0, concat_axis=0, tiled=True, axi...  37.8 us
    all_gather x1, blocking collectives, per_device(): rates = lax.all_gather(conductive_number, 'wall', axis=1, tiled=True)  10.4 us
    all_to_all x1, starting transfers between devices, exchange(): lax.all_to_all(blocks, AXES, split_axis=0, concat_axis=0, tiled=True, axi...  7.11 us
    pallas_call x1, Pallas kernels, with_kernels(): pl.pallas_call(y_forward_kernel, in_specs=[ANY] * 2, out_specs=[ANY, VMEM...  4.97 us
    pallas_call x1, Pallas kernels, with_kernels(): pl.pallas_call(functools.partial(x_kernel, walls), in_specs=[pl.BlockSpec...  4.91 us
    pallas_call x1, Pallas kernels, with_kernels(): pl.pallas_call(functools.partial(y_inverse_kernel, 1.0 / (length * lines...  3.21 us
  transfers between devices with their start and end apart: 1, of which 1 were waited for; matrix products, arithmetic and copies ran while one was open for 0% of the time, Pallas kernels for 0%

profile of v8, /device:TPU:1, one launch (start us, length us, event | category | flops | bytes accessed | tf_op | source)
XLA Modules:
  0.0 120.3 jit_solution(3269498874929799883)
XLA Ops:
  0.0 5.0 %y_forward.1 = (f32[32,2,32,256]{3,2,1,0:T(8,128)}, bf16[2,512,512]{2,1,0:T(8,128)(2,1)S(1)}) custom-call(f32[2,4,64,1024]{3,2,1,0:T(8,128)} %field_hbm.1, bf16[2,6656,512]{2,1,0:T(8,128)(2,1)} %constant.65.clone.table_hbm), custom_call_target="tpu_custom_call" | custom-call | flops 1207959552 | bytes 4194304 | tf_op jit(solution)/shard_map/y_forward/pallas_call | solution.py:294
  5.0 0.0 copy-start
  5.0 7.1 %all-to-all-start = ((f32[32,2,32,256]{3,2,1,0:T(8,128)}), f32[32,2,32,256]{3,2,1,0:T(8,128)S(1)}, u32[]{:S(2)}, u32[]{:S(2)}) async-start(f32[32,2,32,256]{3,2,1,0:T(8,128)} %get-tuple-element.8), calls=%async_computation | async-start | bytes 4194304 | tf_op jit(solution)/shard_map/all_to_all | solution.py:345
  12.1 0.0 copy-done
  12.1 10.4 %all-gather = f32[2,4,2]{1,2,0:T(2,128)S(1)} all-gather(f32[1,4,2]{1,2,0:T(2,128)S(1)} %bitcast.7), channel_id=1, replica_groups=mesh['wall'=2,'row'=16] {'wall'}, dimensions={0}, use_global_device_ids=true | all-gather | bytes 96 | tf_op jit(solution)/shard_map/all_gather | solution.py:403
  22.5 0.1 reshape.126
  22.6 37.8 %all-to-all-done.received_ref = f32[32,2,32,256]{3,2,1,0:T(8,128)S(1)} async-done(((f32[32,2,32,256]{3,2,1,0:T(8,128)}), f32[32,2,32,256]{3,2,1,0:T(8,128)S(1)}, u32[]{:S(2)}, u32[]{:S(2)}) %all-to-all-start) | async-done | bytes 2097184 | tf_op jit(solution)/shard_map/all_to_all | solution.py:345
  60.4 4.9 %x_filter.1 = f32[32,2,32,256]{3,2,1,0:T(8,128)S(1)} custom-call(f32[2,8]{1,0:T(2,128)S(1)} %bitcast.6, f32[32,1]{1,0:T(8,128)S(1)} %fusion.2.square_y_ref, f32[1,1024]{1,0:T(1,128)S(1)} %fusion.11.square_x_ref, bf16[2,512,512]{2,1,0:T(8,128)(2,1)S(1)} %get-tuple-element.7.odd_ref, f32[32,2,32,256]{3,2,1,0:T(8,128)S(1)} %all-to-all-done.received_ref, ...), custom_call_target="tpu_custom_call" | custom-call | flops 2415919104 | bytes 4194304 | tf_op jit(solution)/shard_map/x_filter/pallas_call | solution.py:311
  65.3 51.8 %all_to_all.10.spectrum_ref = f32[32,2,32,256]{3,2,1,0:T(8,128)S(1)} all-to-all(f32[32,2,32,256]{3,2,1,0:T(8,128)S(1)} %x_filter.1), channel_id=1, replica_groups={{0,4,8,12,1,5,9,13,2,6,10,14,3,7,11,15,16,20,24,28,17,21,25,29,18,22,26..., dimensions={0} | all-to-all | bytes 4194304 | tf_op jit(solution)/shard_map/all_to_all | solution.py:345
  117.1 3.2 %y_inverse.1 = f32[2,4,64,1024]{3,2,1,0:T(8,128)} custom-call(bf16[2,512,512]{2,1,0:T(8,128)(2,1)S(1)} %get-tuple-element.7.odd_ref, f32[32,2,32,256]{3,2,1,0:T(8,128)S(1)} %all_to_all.10.spectrum_ref, bf16[2,6656,512]{2,1,0:T(8,128)(2,1)} %constant.65.clone.table_hbm), custom_call_target="tpu_custom_call" | custom-call | flops 1207959552 | bytes 4194304 | tf_op jit(solution)/shard_map/y_inverse/pallas_call | solution.py:325
  (3 shorter events, 0.0 us)
Async XLA Ops:
  5.0 7.1 %copy-start = (f32[2,4]{1,0:T(2,128)S(1)}, f32[2,4]{1,0:T(2,128)}, u32[]{:S(2)}) copy-start(f32[2,4]{1,0:T(2,128)} %param.4) | copy-start | bytes 100
  5.0 55.4 %all-to-all-start = ((f32[32,2,32,256]{3,2,1,0:T(8,128)}), f32[32,2,32,256]{3,2,1,0:T(8,128)S(1)}, u32[]{:S(2)}, u32[]{:S(2)}) async-start(f32[32,2,32,256]{3,2,1,0:T(8,128)} %get-tuple-element.8), calls=%async_computation | async-start | bytes 4194304 | tf_op jit(solution)/shard_map/all_to_all | solution.py:345

commit v9 on v8

--- a/solution.py
+++ b/solution.py
@@ -211,11 +211,9 @@
                     columns = slice(quarter * q + 128 * i, quarter * q + 128 * (i + 1))
                     line_ref[top : top + waves, columns] = a
                     line_ref[top + waves : top + 2 * waves, columns] = b
-        for p in (2, 0, 1):
-            low, high = ranges[p]
-            if s == 0 and p == 0:
-                even_load.wait()
-            table = part_tables(even_ref, odd_ref)[p]
+        if s == 0:
+            even_load.wait()
+        for table, (low, high) in zip(part_tables(even_ref, odd_ref), ranges):
             line_ref[:, low:high] = product(split(line_ref[:, low:high]), table, NT)
 
     def diffuse(s):

time: 121 us -> 121 us (level)
  no operation moved by 1% of the time
where the time goes in v9:
time: 121 us
  blocking collectives  62.2 us (51%)
  waiting for transfers between devices  37.8 us (31%)
  Pallas kernels  13.4 us (11%)
  starting transfers between devices  7.11 us (6%)
    all_to_all x1, blocking collectives, exchange(): lax.all_to_all(blocks, AXES, split_axis=0, concat_axis=0, tiled=True, axi...  51.8 us
    all_to_all x1, waiting for transfers between devices, exchange(): lax.all_to_all(blocks, AXES, split_axis=0, concat_axis=0, tiled=True, axi...  37.8 us
    all_gather x1, blocking collectives, per_device(): rates = lax.all_gather(conductive_number, 'wall', axis=1, tiled=True)  10.4 us
    all_to_all x1, starting transfers between devices, exchange(): lax.all_to_all(blocks, AXES, split_axis=0, concat_axis=0, tiled=True, axi...  7.11 us
    pallas_call x1, Pallas kernels, with_kernels(): pl.pallas_call(functools.partial(x_kernel, walls), in_specs=[pl.BlockSpec...  5.25 us
    pallas_call x1, Pallas kernels, with_kernels(): pl.pallas_call(y_forward_kernel, in_specs=[ANY] * 2, out_specs=[ANY, VMEM...  4.97 us
    pallas_call x1, Pallas kernels, with_kernels(): pl.pallas_call(functools.partial(y_inverse_kernel, 1.0 / (length * lines...  3.21 us
  transfers between devices with their start and end apart: 1, of which 1 were waited for; matrix products, arithmetic and copies ran while one was open for 0% of the time, Pallas kernels for 0%

profile of v9, /device:TPU:1, one launch (start us, length us, event | category | flops | bytes accessed | tf_op | source)
XLA Modules:
  0.0 120.6 jit_solution(17175351708089274087)
XLA Ops:
  0.0 5.0 %y_forward.1 = (f32[32,2,32,256]{3,2,1,0:T(8,128)}, bf16[2,512,512]{2,1,0:T(8,128)(2,1)S(1)}) custom-call(f32[2,4,64,1024]{3,2,1,0:T(8,128)} %field_hbm.1, bf16[2,6656,512]{2,1,0:T(8,128)(2,1)} %constant.65.clone.table_hbm), custom_call_target="tpu_custom_call" | custom-call | flops 1207959552 | bytes 4194304 | tf_op jit(solution)/shard_map/y_forward/pallas_call | solution.py:292
  5.0 0.0 copy-start
  5.0 7.1 %all-to-all-start = ((f32[32,2,32,256]{3,2,1,0:T(8,128)}), f32[32,2,32,256]{3,2,1,0:T(8,128)S(1)}, u32[]{:S(2)}, u32[]{:S(2)}) async-start(f32[32,2,32,256]{3,2,1,0:T(8,128)} %get-tuple-element.8), calls=%async_computation | async-start | bytes 4194304 | tf_op jit(solution)/shard_map/all_to_all | solution.py:343
  12.1 0.0 copy-done
  12.1 10.4 %all-gather = f32[2,4,2]{1,2,0:T(2,128)S(1)} all-gather(f32[1,4,2]{1,2,0:T(2,128)S(1)} %bitcast.7), channel_id=1, replica_groups=mesh['wall'=2,'row'=16] {'wall'}, dimensions={0}, use_global_device_ids=true | all-gather | bytes 96 | tf_op jit(solution)/shard_map/all_gather | solution.py:401
  22.5 0.1 reshape.126
  22.6 37.8 %all-to-all-done.received_ref = f32[32,2,32,256]{3,2,1,0:T(8,128)S(1)} async-done(((f32[32,2,32,256]{3,2,1,0:T(8,128)}), f32[32,2,32,256]{3,2,1,0:T(8,128)S(1)}, u32[]{:S(2)}, u32[]{:S(2)}) %all-to-all-start) | async-done | bytes 2097184 | tf_op jit(solution)/shard_map/all_to_all | solution.py:343
  60.4 5.3 %x_filter.1 = f32[32,2,32,256]{3,2,1,0:T(8,128)S(1)} custom-call(f32[2,8]{1,0:T(2,128)S(1)} %bitcast.6, f32[32,1]{1,0:T(8,128)S(1)} %fusion.2.square_y_ref, f32[1,1024]{1,0:T(1,128)S(1)} %fusion.11.square_x_ref, bf16[2,512,512]{2,1,0:T(8,128)(2,1)S(1)} %get-tuple-element.7.odd_ref, f32[32,2,32,256]{3,2,1,0:T(8,128)S(1)} %all-to-all-done.received_ref, ...), custom_call_target="tpu_custom_call" | custom-call | flops 2415919104 | bytes 4194304 | tf_op jit(solution)/shard_map/x_filter/pallas_call | solution.py:309
  65.6 51.8 %all_to_all.10.spectrum_ref = f32[32,2,32,256]{3,2,1,0:T(8,128)S(1)} all-to-all(f32[32,2,32,256]{3,2,1,0:T(8,128)S(1)} %x_filter.1), channel_id=1, replica_groups={{0,4,8,12,1,5,9,13,2,6,10,14,3,7,11,15,16,20,24,28,17,21,25,29,18,22,26..., dimensions={0} | all-to-all | bytes 4194304 | tf_op jit(solution)/shard_map/all_to_all | solution.py:343
  117.4 3.2 %y_inverse.1 = f32[2,4,64,1024]{3,2,1,0:T(8,128)} custom-call(bf16[2,512,512]{2,1,0:T(8,128)(2,1)S(1)} %get-tuple-element.7.odd_ref, f32[32,2,32,256]{3,2,1,0:T(8,128)S(1)} %all_to_all.10.spectrum_ref, bf16[2,6656,512]{2,1,0:T(8,128)(2,1)} %constant.65.clone.table_hbm), custom_call_target="tpu_custom_call" | custom-call | flops 1207959552 | bytes 4194304 | tf_op jit(solution)/shard_map/y_inverse/pallas_call | solution.py:323
  (3 shorter events, 0.0 us)
Async XLA Ops:
  5.0 7.1 %copy-start = (f32[2,4]{1,0:T(2,128)S(1)}, f32[2,4]{1,0:T(2,128)}, u32[]{:S(2)}) copy-start(f32[2,4]{1,0:T(2,128)} %param.4) | copy-start | bytes 100
  5.0 55.4 %all-to-all-start = ((f32[32,2,32,256]{3,2,1,0:T(8,128)}), f32[32,2,32,256]{3,2,1,0:T(8,128)S(1)}, u32[]{:S(2)}, u32[]{:S(2)}) async-start(f32[32,2,32,256]{3,2,1,0:T(8,128)} %get-tuple-element.8), calls=%async_computation | async-start | bytes 4194304 | tf_op jit(solution)/shard_map/all_to_all | solution.py:343

commit v10 on v8

--- a/solution.py
+++ b/solution.py
@@ -138,25 +138,17 @@
         store.wait()
 
 
-def y_inverse_kernel(
-    norm, odd_ref, spectrum_ref, table_hbm, out_hbm, even_ref, out_ref, table_sem, out_sem
-):
-    even_load = even_copy(table_hbm, even_ref, table_sem.at[0])
-    even_load.start()
+def y_inverse_kernel(norm, even_ref, odd_ref, spectrum_ref, out_hbm, out_ref, out_sem):
     devices, scalars, waves, rows = spectrum_ref.shape
     planes, lines, length = out_ref.shape[1:]
     quarter = length // 4
     ranges = part_ranges(devices)
     stores = []
     for s in range(scalars):
-        parts = {}
-        for p in (2, 0, 1):
-            low, high = ranges[p]
-            turned = split(spectrum_ref[low:high, s].reshape(-1, rows).T)
-            if s == 0 and p == 0:
-                even_load.wait()
-            parts[p] = product(turned, part_tables(even_ref, odd_ref)[p], NN)
-        first, second, third = (parts[p] for p in range(3))
+        first, second, third = (
+            product(split(spectrum_ref[low:high, s].reshape(-1, rows).T), table, NN)
+            for table, (low, high) in zip(part_tables(even_ref, odd_ref), ranges)
+        )
         quarters = unfold(first * norm, second * norm, third[:, :quarter] * norm, third[:, quarter:] * norm)
         for q, value in enumerate(quarters):
             out_ref[s, :, :, q * quarter : (q + 1) * quarter] = value.reshape(planes, lines, quarter)
@@ -308,35 +300,32 @@
         cost_estimate=cost(work, total),
         name="y_forward",
     )(fields, table)
-    filtered = pl.pallas_call(
+    filtered, even = pl.pallas_call(
         functools.partial(x_kernel, walls),
         in_specs=[pl.BlockSpec(memory_space=pltpu.SMEM)] + [VMEM] * 4 + [ANY],
-        out_specs=VMEM,
-        out_shape=blocks,
+        out_specs=[VMEM] * 2,
+        out_shape=[blocks, jax.ShapeDtypeStruct(even_scratch.shape, jnp.bfloat16)],
         scratch_shapes=[
-            even_scratch,
             pltpu.SemaphoreType.DMA((1,)),
             *[pltpu.VMEM((walls * planes * waves, lines * groups), jnp.float32)] * scalars,
         ],
-        compiler_params=grant(48),
+        compiler_params=grant(46),
         cost_estimate=cost(2 * work, total),
         name="x_filter",
     )(rates, square_y, square_x, odd, exchange(spectrum), table)
     return pl.pallas_call(
         functools.partial(y_inverse_kernel, 1.0 / (length * lines * groups)),
-        in_specs=[VMEM] * 2 + [ANY],
+        in_specs=[VMEM] * 3,
         out_specs=ANY,
         out_shape=jax.ShapeDtypeStruct(fields.shape, jnp.float32),
         scratch_shapes=[
-            even_scratch,
             pltpu.VMEM(fields.shape, jnp.float32),
-            pltpu.SemaphoreType.DMA((1,)),
             pltpu.SemaphoreType.DMA((scalars, planes)),
         ],
         compiler_params=grant(48),
         cost_estimate=cost(work, total),
         name="y_inverse",
-    )(odd, exchange(filtered), table)
+    )(even, odd, exchange(filtered))
 
 
 def exchange(blocks):

time: 121 us -> 120 us (level)
  no operation moved by 1% of the time
where the time goes in v10:
time: 120 us
  blocking collectives  62.2 us (52%)
  waiting for transfers between devices  37.8 us (31%)
  Pallas kernels  12.5 us (10%)
  starting transfers between devices  7.11 us (6%)
    all_to_all x1, blocking collectives, exchange(): lax.all_to_all(blocks, AXES, split_axis=0, concat_axis=0, tiled=True, axi...  51.8 us
    all_to_all x1, waiting for transfers between devices, exchange(): lax.all_to_all(blocks, AXES, split_axis=0, concat_axis=0, tiled=True, axi...  37.8 us
    all_gather x1, blocking collectives, per_device(): rates = lax.all_gather(conductive_number, 'wall', axis=1, tiled=True)  10.4 us
    all_to_all x1, starting transfers between devices, exchange(): lax.all_to_all(blocks, AXES, split_axis=0, concat_axis=0, tiled=True, axi...  7.11 us
    pallas_call x1, Pallas kernels, with_kernels(): pl.pallas_call(y_forward_kernel, in_specs=[ANY] * 2, out_specs=[ANY, VMEM...  4.97 us
    pallas_call x1, Pallas kernels, with_kernels(): pl.pallas_call(functools.partial(x_kernel, walls), in_specs=[pl.BlockSpec...  4.91 us
    pallas_call x1, Pallas kernels, with_kernels(): pl.pallas_call(functools.partial(y_inverse_kernel, 1.0 / (length * lines...  2.68 us
  transfers between devices with their start and end apart: 1, of which 1 were waited for; matrix products, arithmetic and copies ran while one was open for 0% of the time, Pallas kernels for 0%

profile of v10, /device:TPU:1, one launch (start us, length us, event | category | flops | bytes accessed | tf_op | source)
XLA Modules:
  0.0 119.7 jit_solution(3323347253879343610)
XLA Ops:
  0.0 5.0 %y_forward.1 = (f32[32,2,32,256]{3,2,1,0:T(8,128)}, bf16[2,512,512]{2,1,0:T(8,128)(2,1)S(1)}) custom-call(f32[2,4,64,1024]{3,2,1,0:T(8,128)} %field_hbm.1, bf16[2,6656,512]{2,1,0:T(8,128)(2,1)} %constant.65.clone.table_hbm), custom_call_target="tpu_custom_call" | custom-call | flops 1207959552 | bytes 4194304 | tf_op jit(solution)/shard_map/y_forward/pallas_call | solution.py:286
  5.0 0.0 copy-start
  5.0 7.1 %all-to-all-start = ((f32[32,2,32,256]{3,2,1,0:T(8,128)}), f32[32,2,32,256]{3,2,1,0:T(8,128)S(1)}, u32[]{:S(2)}, u32[]{:S(2)}) async-start(f32[32,2,32,256]{3,2,1,0:T(8,128)} %get-tuple-element.10), calls=%async_computation | async-start | bytes 4194304 | tf_op jit(solution)/shard_map/all_to_all | solution.py:334
  12.1 0.0 copy-done
  12.1 10.4 %all-gather = f32[2,4,2]{1,2,0:T(2,128)S(1)} all-gather(f32[1,4,2]{1,2,0:T(2,128)S(1)} %bitcast.7), channel_id=1, replica_groups=mesh['wall'=2,'row'=16] {'wall'}, dimensions={0}, use_global_device_ids=true | all-gather | bytes 96 | tf_op jit(solution)/shard_map/all_gather | solution.py:392
  22.5 0.1 reshape.126
  22.6 37.8 %all-to-all-done.received_ref = f32[32,2,32,256]{3,2,1,0:T(8,128)S(1)} async-done(((f32[32,2,32,256]{3,2,1,0:T(8,128)}), f32[32,2,32,256]{3,2,1,0:T(8,128)S(1)}, u32[]{:S(2)}, u32[]{:S(2)}) %all-to-all-start) | async-done | bytes 2097184 | tf_op jit(solution)/shard_map/all_to_all | solution.py:334
  60.4 4.9 %x_filter.1 = (f32[32,2,32,256]{3,2,1,0:T(8,128)S(1)}, bf16[2,256,512]{2,1,0:T(8,128)(2,1)S(1)}) custom-call(f32[2,8]{1,0:T(2,128)S(1)} %bitcast.6, f32[32,1]{1,0:T(8,128)S(1)} %fusion.2.square_y_ref, f32[1,1024]{1,0:T(1,128)S(1)} %fusion.11.square_x_ref, bf16[2,512,512]{2,1,0:T(8,128)(2,1)S(1)} %get-tuple-element.9.odd_ref, ...), custom_call_target="tpu_custom_call" | custom-call | flops 2415919104 | bytes 4194304 | tf_op jit(solution)/shard_map/x_filter/pallas_call | solution.py:303
  65.3 51.8 %all_to_all.10.spectrum_ref = f32[32,2,32,256]{3,2,1,0:T(8,128)S(1)} all-to-all(f32[32,2,32,256]{3,2,1,0:T(8,128)S(1)} %get-tuple-element.12), channel_id=1, replica_groups={{0,4,8,12,1,5,9,13,2,6,10,14,3,7,11,15,16,20,24,28,17,21,25,29,18,22,26..., dimensions={0} | all-to-all | bytes 4194304 | tf_op jit(solution)/shard_map/all_to_all | solution.py:334
  117.1 2.7 %y_inverse.1 = f32[2,4,64,1024]{3,2,1,0:T(8,128)} custom-call(bf16[2,256,512]{2,1,0:T(8,128)(2,1)S(1)} %get-tuple-element.11.even_ref, bf16[2,512,512]{2,1,0:T(8,128)(2,1)S(1)} %get-tuple-element.9.odd_ref, f32[32,2,32,256]{3,2,1,0:T(8,128)S(1)} %all_to_all.10.spectrum_ref), custom_call_target="tpu_custom_call" | custom-call | flops 1207959552 | bytes 4194304 | tf_op jit(solution)/shard_map/y_inverse/pallas_call | solution.py:316
  (3 shorter events, 0.0 us)
Async XLA Ops:
  5.0 7.1 %copy-start = (f32[2,4]{1,0:T(2,128)S(1)}, f32[2,4]{1,0:T(2,128)}, u32[]{:S(2)}) copy-start(f32[2,4]{1,0:T(2,128)} %param.4) | copy-start | bytes 100
  5.0 55.4 %all-to-all-start = ((f32[32,2,32,256]{3,2,1,0:T(8,128)}), f32[32,2,32,256]{3,2,1,0:T(8,128)S(1)}, u32[]{:S(2)}, u32[]{:S(2)}) async-start(f32[32,2,32,256]{3,2,1,0:T(8,128)} %get-tuple-element.10), calls=%async_computation | async-start | bytes 4194304 | tf_op jit(solution)/shard_map/all_to_all | solution.py:334

commit v11 on v4

--- a/solution.py
+++ b/solution.py
@@ -220,18 +220,19 @@
             columns = slice(128 * j, 128 * (j + 1))
             square_x = square_x_ref[:, columns]
             damping = [jnp.exp(-rate * square_x) * dy for rate, dy in zip(rates, damping_y)]
+            own = [d * (1.0 - 2.0 * rate) for d, rate in zip(damping, rates)]
+            share = [d * rate for d, rate in zip(damping, rates)]
             field = [line_ref[z * waves : (z + 1) * waves, columns] for z in range(count)]
             for step in range(STEPS):
                 updated = []
                 for z in range(count):
-                    value = (1.0 - 2.0 * rates[z]) * field[z]
                     if z == 0:
                         around = field[1]
                     elif z == count - 1:
                         around = field[z - 1]
                     else:
                         around = field[z - 1] + field[z + 1]
-                    updated.append(damping[z] * (value + rates[z] * around))
+                    updated.append(own[z] * field[z] + share[z] * around)
                 field = updated
             for z in range(count):
                 line_ref[z * waves : (z + 1) * waves, columns] = field[z]

time: 120 us -> 121 us (level)
  no operation moved by 1% of the time
where the time goes in v11:
time: 121 us; the launch traced here: 120 us
  blocking collectives  62.2 us (51%)
  waiting for transfers between devices  35.6 us (29%)
  Pallas kernels  14.4 us (12%)
  starting transfers between devices  7.16 us (6%)
    all_to_all x1, blocking collectives, exchange(): lax.all_to_all(blocks, AXES, split_axis=0, concat_axis=0, tiled=True, axi...  51.8 us
    all_to_all x1, waiting for transfers between devices, exchange(): lax.all_to_all(blocks, AXES, split_axis=0, concat_axis=0, tiled=True, axi...  35.6 us
    all_gather x1, blocking collectives, per_device(): rates = lax.all_gather(conductive_number, 'wall', axis=1, tiled=True)  10.4 us
    all_to_all x1, starting transfers between devices, exchange(): lax.all_to_all(blocks, AXES, split_axis=0, concat_axis=0, tiled=True, axi...  7.16 us
    pallas_call x1, Pallas kernels, with_kernels(): pl.pallas_call(functools.partial(x_kernel, walls), in_specs=[pl.BlockSpec...  5.35 us
    pallas_call x1, Pallas kernels, with_kernels(): pl.pallas_call(y_forward_kernel, in_specs=[ANY] * 2, out_specs=ANY, out_s...  4.97 us
    pallas_call x1, Pallas kernels, with_kernels(): pl.pallas_call(functools.partial(y_inverse_kernel, 1.0 / (length * lines...  2.67 us
  transfers between devices with their start and end apart: 1, of which 1 were waited for; matrix products, arithmetic and copies ran while one was open for 1% of the time, Pallas kernels for 1%

profile of v11, /device:TPU:1, one launch (start us, length us, event | category | flops | bytes accessed | tf_op | source)
XLA Modules:
  0.0 120.3 jit_solution(8692175895741519159)
XLA Ops:
  0.0 5.0 %y_forward.1 = f32[32,2,32,256]{3,2,1,0:T(8,128)} custom-call(f32[2,4,64,1024]{3,2,1,0:T(8,128)} %field_hbm.1, bf16[2,6656,512]{2,1,0:T(8,128)(2,1)} %constant.65.clone.table_hbm), custom_call_target="tpu_custom_call" | custom-call | flops 1207959552 | bytes 4194304 | tf_op jit(solution)/shard_map/y_forward/pallas_call | solution.py:287
  5.0 0.0 copy-start
  5.0 7.2 %all-to-all-start = ((f32[32,2,32,256]{3,2,1,0:T(8,128)}), f32[32,2,32,256]{3,2,1,0:T(8,128)}, u32[]{:S(2)}, u32[]{:S(2)}) async-start(f32[32,2,32,256]{3,2,1,0:T(8,128)} %y_forward.1), calls=%async_computation | async-start | bytes 4194304 | tf_op jit(solution)/shard_map/all_to_all | solution.py:342
  12.2 0.0 copy-done
  12.2 10.4 %all-gather = f32[2,4,2]{1,2,0:T(2,128)S(1)} all-gather(f32[1,4,2]{1,2,0:T(2,128)S(1)} %bitcast.9), channel_id=1, replica_groups=mesh['wall'=2,'row'=16] {'wall'}, dimensions={0}, use_global_device_ids=true | all-gather | bytes 96 | tf_op jit(solution)/shard_map/all_gather | solution.py:400
  22.6 0.1 reshape.126
  22.7 0.7 slice_bitcast_fusion.after_hbm
  23.4 1.4 %hold.1.table_ref = bf16[2,768,512]{2,1,0:T(8,128)(2,1)S(1)} custom-call(f32[8,128]{1,0:T(8,128)S(1)} %slice_bitcast_fusion.after_hbm, bf16[2,6656,512]{2,1,0:T(8,128)(2,1)} %constant.65.clone.table_hbm), custom_call_target="tpu_custom_call" | custom-call | bytes 2097152 | tf_op jit(solution)/shard_map/hold/pallas_call | solution.py:304
  24.8 35.6 %all-to-all-done.received_ref = f32[32,2,32,256]{3,2,1,0:T(8,128)} async-done(((f32[32,2,32,256]{3,2,1,0:T(8,128)}), f32[32,2,32,256]{3,2,1,0:T(8,128)}, u32[]{:S(2)}, u32[]{:S(2)}) %all-to-all-start) | async-done | bytes 2097184 | tf_op jit(solution)/shard_map/all_to_all | solution.py:342
  60.5 5.3 %x_filter.1 = f32[32,2,32,256]{3,2,1,0:T(8,128)S(1)} custom-call(f32[2,8]{1,0:T(2,128)S(1)} %bitcast.8, f32[32,1]{1,0:T(8,128)S(1)} %fusion.2.square_y_ref, f32[1,1024]{1,0:T(1,128)S(1)} %fusion.11.square_x_ref, bf16[2,768,512]{2,1,0:T(8,128)(2,1)S(1)} %hold.1.table_ref, f32[32,2,32,256]{3,2,1,0:T(8,128)} %all-to-all-done.received_ref), custom_call_target="tpu_custom_call" | custom-call | flops 2415919104 | bytes 4194304 | tf_op jit(solution)/shard_map/x_filter/pallas_call | solution.py:314
  65.8 51.8 %all_to_all.10.spectrum_ref = f32[32,2,32,256]{3,2,1,0:T(8,128)S(1)} all-to-all(f32[32,2,32,256]{3,2,1,0:T(8,128)S(1)} %x_filter.1), channel_id=1, replica_groups={{0,4,8,12,1,5,9,13,2,6,10,14,3,7,11,15,16,20,24,28,17,21,25,29,18,22,26..., dimensions={0} | all-to-all | bytes 4194304 | tf_op jit(solution)/shard_map/all_to_all | solution.py:342
  117.6 2.7 %y_inverse.1 = f32[2,4,64,1024]{3,2,1,0:T(8,128)} custom-call(bf16[2,768,512]{2,1,0:T(8,128)(2,1)S(1)} %hold.1.table_ref, f32[32,2,32,256]{3,2,1,0:T(8,128)S(1)} %all_to_all.10.spectrum_ref), custom_call_target="tpu_custom_call" | custom-call | flops 1207959552 | bytes 4194304 | tf_op jit(solution)/shard_map/y_inverse/pallas_call | solution.py:324
  (3 shorter events, 0.0 us)
Async XLA Ops:
  5.0 7.2 %copy-start = (f32[2,4]{1,0:T(2,128)S(1)}, f32[2,4]{1,0:T(2,128)}, u32[]{:S(2)}) copy-start(f32[2,4]{1,0:T(2,128)} %param.4) | copy-start | bytes 100
  5.0 55.5 %all-to-all-start = ((f32[32,2,32,256]{3,2,1,0:T(8,128)}), f32[32,2,32,256]{3,2,1,0:T(8,128)}, u32[]{:S(2)}, u32[]{:S(2)}) async-start(f32[32,2,32,256]{3,2,1,0:T(8,128)} %y_forward.1), calls=%async_computation | async-start | bytes 4194304 | tf_op jit(solution)/shard_map/all_to_all | solution.py:342
